TPU v7x, 32 devices: a whole 2x2x4 slice. The times are simulated.
32 devices in a mesh: inp: 8 (over y, x, core), tm: 4 (over z).
Axes of the slice: x: 2, y: 2, z: 4, core: 2. Of those that a mesh axis runs over, the one named last changes fastest.
Arguments:
- voltages: bfloat16 [1024, 262144], P('inp', 'tm'), may hold values from -6 to 6
- prototype: float32 [8, 1024], replicated, may hold values from -2 to 2
Outputs:
- correlation: bfloat16 [512, 2, 1024, 1024], P(('inp', 'tm'))
All inputs are finite; a program needn't handle non-finite values.
Results may differ from a plain program's by a relative error of at most 0.0065.
Values may be sent and summed in bfloat16 or wider, within the bound.
No kernel may reach another device: no remote copies, remote signals or barrier semaphores. Data moves between devices by JAX's collectives and lax.ppermute only.
A program may use at most 192 MiB of HBM per device.

v0:
```python
import math

import jax
import jax.numpy as jnp
from jax import lax
from jax.sharding import PartitionSpec as P

TAPS = 8
SPEC_DEV = 64
FRAME = 1024


def shifted(block, axis, distance):
    devices = range(lax.axis_size(axis))
    route = [(i - distance, i) for i in devices if i - distance in devices]
    return lax.ppermute(block, axis, route)


def dft_table(frame):
    sample = jnp.arange(frame, dtype=jnp.int32)[:, None]
    column = jnp.arange(frame, dtype=jnp.int32)[None, :]
    phase = (sample * (column // 2) % frame).astype(jnp.float32) * (2.0 * math.pi / frame)
    table = jnp.where(column % 2 == 0, jnp.cos(phase), -jnp.sin(phase))
    return table.astype(jnp.bfloat16)


def channelize(frames, earlier, prototype):
    count = frames.shape[1]
    joined = jnp.concatenate([earlier, frames], axis=1)
    filtered = jnp.zeros(frames.shape, jnp.float32)
    for tap_index in range(TAPS):
        filtered = filtered + prototype[tap_index] * joined[
            :, tap_index : tap_index + count, :
        ].astype(jnp.float32)
    filtered = filtered.astype(jnp.bfloat16)
    dims = (((0,), (2,)), ((), ()))
    spectra = lax.dot_general(
        dft_table(frames.shape[2]), filtered, dims, preferred_element_type=jnp.float32
    )
    return spectra.astype(jnp.bfloat16)


def correlate(planes):
    real_part = planes[0]
    imag_part = planes[1]
    dims = (((1,), (1,)), ((), ()))
    real_real = lax.dot_general(real_part, real_part, dims, preferred_element_type=jnp.float32)
    imag_imag = lax.dot_general(imag_part, imag_part, dims, preferred_element_type=jnp.float32)
    imag_real = lax.dot_general(imag_part, real_part, dims, preferred_element_type=jnp.float32)
    real_gram = real_real + imag_imag
    imag_gram = imag_real - imag_real.T
    scales = lax.rsqrt(jnp.diagonal(real_gram) + 1e-06)
    outer = scales[:, None] * scales[None, :]
    return jnp.stack([real_gram * outer, imag_gram * outer]).astype(jnp.bfloat16)


def shards(voltages, prototype):
    inputs_here = voltages.shape[0]
    frames = voltages.reshape(inputs_here, SPEC_DEV, FRAME)
    earlier = shifted(frames[:, SPEC_DEV - TAPS + 1 :, :], "tm", 1)
    spectra = channelize(frames, earlier, prototype)
    groups_inp = lax.axis_size("inp")
    groups_tm = lax.axis_size("tm")
    width = FRAME // (groups_inp * groups_tm)
    turned = lax.all_to_all(
        lax.all_to_all(spectra, "inp", split_axis=0, concat_axis=1, tiled=True),
        "tm",
        split_axis=0,
        concat_axis=2,
        tiled=True,
    )
    channels_here = width // 2
    planes = turned.reshape(channels_here, 2, turned.shape[1], turned.shape[2])
    return lax.map(correlate, planes)


def solution(mesh):
    return jax.shard_map(
        shards,
        mesh=mesh,
        in_specs=(P("inp", "tm"), P()),
        out_specs=P(("inp", "tm"), None, None, None),
        check_vma=False,
    )
```

profile of v0, /device:TPU:0, one launch (start us, length us, event | category | flops | bytes accessed | tf_op | source)
XLA Modules:
  0.0 1449.6 jit_solution(9198634553255089580)
XLA Ops:
  0.0 10.3 copy.56
  15.9 18.5 %fusion.39 = bf16[1024,1024,1]{0,1,2:T(8,128)(2,1)S(1)} fusion(s32[1024]{0:T(1024)S(1)} %add_select_fusion.1, pred[1024]{0:T(1024)(128)(4,1)S(1)} %fusion.25), kind=kLoop, calls=%fused_computation.33.clone.clone.2 | loop fusion | flops 17825792 | bytes 2102272 | tf_op jit(solution)/shard_map/dot_general | solution.py:37
  34.5 20.5 %collective-permute-done = bf16[128,7,1024]{2,0,1:T(8,128)(2,1)S(1)} collective-permute-done((bf16[128,7,1024]{2,0,1:T(8,128)(2,1)S(1)}, bf16[128,7,1024]{2,0,1:T(8,128)(2,1)S(1)}, u32[]{:S(2)}, u32[]{:S(2)}) %collective-permute-start) | collective-permute-done | bytes 1835040 | tf_op jit(solution)/shard_map/ppermute | solution.py:16
  57.7 6.8 copy-done
  64.5 54.0 %fusion.10 = bf16[1024,128,64]{1,0,2:T(8,128)(2,1)} fusion(bf16[128,71,1024]{2,0,1:T(8,128)(2,1)} %copy-done, f32[1024]{0:T(1024)S(1)} %bitcast.89, f32[1024]{0:T(1024)S(1)} %bitcast.90, f32[1024]{0:T(1024)S(1)} %bitcast.84, f32[1024]{0:T(1024)S(1)} %bitcast.85, f32[1024]{0:T(1024)S(1)} %bitcast.86, f32[1024]{0:T(1024)S(1)} %bitcast.87, ...), kind=kOutput, calls=%fused_computation.22 | convolution fusion | flops 17389584384 | bytes 153124864 | tf_op jit(solution)/shard_map/dot_general | solution.py:37
  118.5 14.8 %copy.38 = bf16[1024,128,64]{1,2,0:T(8,128)(2,1)S(1)} copy(bf16[1024,128,64]{1,0,2:T(8,128)(2,1)} %fusion.10) | data formatting | bytes 33554432 | tf_op jit(solution)/shard_map/convert_element_type | solution.py:40
  133.3 187.7 %all_to_all.33 = bf16[1024,128,64]{1,2,0:T(8,128)(2,1)} all-to-all(bf16[1024,128,64]{1,2,0:T(8,128)(2,1)S(1)} %copy.38), channel_id=1, replica_groups=mesh['inp'=8,'tm'=4] {'inp'}, dimensions={0} | all-to-all | bytes 33554432 | tf_op jit(solution)/shard_map/all_to_all | solution.py:66
  321.0 25.7 %copy.39 = bf16[128,8,128,64]{0,3,2,1:T(8,128)(2,1)} copy(bf16[128,8,128,64]{2,3,0,1:T(8,128)(2,1)} %bitcast.79) | data formatting | bytes 33554432 | tf_op jit(solution)/shard_map/all_to_all | solution.py:66
  346.7 26.0 %copy.40 = bf16[128,1024,64]{1,2,0:T(8,128)(2,1)} copy(bf16[128,1024,64]{0,2,1:T(8,128)(2,1)} %bitcast.80) | data formatting | bytes 33554432 | tf_op jit(solution)/shard_map/all_to_all | solution.py:66
  372.7 7.2 all-to-all-start.1
  379.8 363.3 %all-to-all-done.1 = bf16[128,1024,64]{1,2,0:T(8,128)(2,1)} async-done(((bf16[128,1024,64]{1,2,0:T(8,128)(2,1)}), bf16[128,1024,64]{1,2,0:T(8,128)(2,1)}, u32[]{:S(2)}, u32[]{:S(2)}) %all-to-all-start.1) | async-done | bytes 16777248 | tf_op jit(solution)/shard_map/all_to_all | solution.py:65
  743.2 14.0 copy.41
  757.2 692.4 %while.10 = (s32[]{:T(128)}, bf16[16,2,1024,1024]{3,2,1,0:T(8,128)(2,1)}, bf16[16,2,1024,256]{2,3,1,0:T(8,128)(2,1)}, s32[]{:T(128)}, s32[]{:T(128)}, /*index=5*/s32[]{}) while((s32[]{:T(128)}, bf16[16,2,1024,1024]{3,2,1,0:T(8,128)(2,1)}, bf16[16,2,1024,256]{2,3,1,0:T(8,128)(2,1)}, s32[]{:T(128)}, s32[]{:T(128)}, /*index=5*/s32[]{}) %tuple.35), condition=%wide.region_1.2_spmd, body=%wide.region_0.1_spmd.sunk | while | flops 1626346496 | bytes 52464216 | solution.py:74
  766.4 16.9 %gather_fusion = f32[1024]{0:T(1024)S(1)} fusion(f32[1024,1024]{1,0:T(8,128)} %convolution_add_fusion.2, s32[1024]{0:T(1024)S(1)} %bitcast.73), kind=kCustom, calls=%fused_computation.clone.1 | custom fusion | bytes 16384 | tf_op jit(solution)/shard_map/while/body/eval_jaxpr/jit(diagonal)/cond/branch_0_fun/gather | solution.py:52
  787.2 5.4 copy.58
  792.5 5.5 fusion.46
  809.6 16.9 %gather_fusion = f32[1024]{0:T(1024)S(1)} fusion(f32[1024,1024]{1,0:T(8,128)} %convolution_add_fusion.2, s32[1024]{0:T(1024)S(1)} %bitcast.73), kind=kCustom, calls=%fused_computation.clone.1 | custom fusion | bytes 16384 | tf_op jit(solution)/shard_map/while/body/eval_jaxpr/jit(diagonal)/cond/branch_0_fun/gather | solution.py:52
  830.4 5.4 copy.58
  835.8 5.5 fusion.46
  852.9 16.9 %gather_fusion = f32[1024]{0:T(1024)S(1)} fusion(f32[1024,1024]{1,0:T(8,128)} %convolution_add_fusion.2, s32[1024]{0:T(1024)S(1)} %bitcast.73), kind=kCustom, calls=%fused_computation.clone.1 | custom fusion | bytes 16384 | tf_op jit(solution)/shard_map/while/body/eval_jaxpr/jit(diagonal)/cond/branch_0_fun/gather | solution.py:52
  873.7 5.4 copy.58
  879.1 5.5 fusion.46
  896.2 16.9 %gather_fusion = f32[1024]{0:T(1024)S(1)} fusion(f32[1024,1024]{1,0:T(8,128)} %convolution_add_fusion.2, s32[1024]{0:T(1024)S(1)} %bitcast.73), kind=kCustom, calls=%fused_computation.clone.1 | custom fusion | bytes 16384 | tf_op jit(solution)/shard_map/while/body/eval_jaxpr/jit(diagonal)/cond/branch_0_fun/gather | solution.py:52
  922.4 5.5 fusion.46
  939.5 16.9 %gather_fusion = f32[1024]{0:T(1024)S(1)} fusion(f32[1024,1024]{1,0:T(8,128)} %convolution_add_fusion.2, s32[1024]{0:T(1024)S(1)} %bitcast.73), kind=kCustom, calls=%fused_computation.clone.1 | custom fusion | bytes 16384 | tf_op jit(solution)/shard_map/while/body/eval_jaxpr/jit(diagonal)/cond/branch_0_fun/gather | solution.py:52
  965.6 5.5 fusion.46
  982.7 16.9 %gather_fusion = f32[1024]{0:T(1024)S(1)} fusion(f32[1024,1024]{1,0:T(8,128)} %convolution_add_fusion.2, s32[1024]{0:T(1024)S(1)} %bitcast.73), kind=kCustom, calls=%fused_computation.clone.1 | custom fusion | bytes 16384 | tf_op jit(solution)/shard_map/while/body/eval_jaxpr/jit(diagonal)/cond/branch_0_fun/gather | solution.py:52
  1008.9 5.5 fusion.46
  1026.0 16.9 %gather_fusion = f32[1024]{0:T(1024)S(1)} fusion(f32[1024,1024]{1,0:T(8,128)} %convolution_add_fusion.2, s32[1024]{0:T(1024)S(1)} %bitcast.73), kind=kCustom, calls=%fused_computation.clone.1 | custom fusion | bytes 16384 | tf_op jit(solution)/shard_map/while/body/eval_jaxpr/jit(diagonal)/cond/branch_0_fun/gather | solution.py:52
  1052.2 5.5 fusion.46
  1069.3 16.9 %gather_fusion = f32[1024]{0:T(1024)S(1)} fusion(f32[1024,1024]{1,0:T(8,128)} %convolution_add_fusion.2, s32[1024]{0:T(1024)S(1)} %bitcast.73), kind=kCustom, calls=%fused_computation.clone.1 | custom fusion | bytes 16384 | tf_op jit(solution)/shard_map/while/body/eval_jaxpr/jit(diagonal)/cond/branch_0_fun/gather | solution.py:52
  1095.5 5.5 fusion.46
  1112.6 16.9 %gather_fusion = f32[1024]{0:T(1024)S(1)} fusion(f32[1024,1024]{1,0:T(8,128)} %convolution_add_fusion.2, s32[1024]{0:T(1024)S(1)} %bitcast.73), kind=kCustom, calls=%fused_computation.clone.1 | custom fusion | bytes 16384 | tf_op jit(solution)/shard_map/while/body/eval_jaxpr/jit(diagonal)/cond/branch_0_fun/gather | solution.py:52
  1138.8 5.5 fusion.46
  1155.8 16.9 %gather_fusion = f32[1024]{0:T(1024)S(1)} fusion(f32[1024,1024]{1,0:T(8,128)} %convolution_add_fusion.2, s32[1024]{0:T(1024)S(1)} %bitcast.73), kind=kCustom, calls=%fused_computation.clone.1 | custom fusion | bytes 16384 | tf_op jit(solution)/shard_map/while/body/eval_jaxpr/jit(diagonal)/cond/branch_0_fun/gather | solution.py:52
  1182.0 5.5 fusion.46
  1199.1 16.9 %gather_fusion = f32[1024]{0:T(1024)S(1)} fusion(f32[1024,1024]{1,0:T(8,128)} %convolution_add_fusion.2, s32[1024]{0:T(1024)S(1)} %bitcast.73), kind=kCustom, calls=%fused_computation.clone.1 | custom fusion | bytes 16384 | tf_op jit(solution)/shard_map/while/body/eval_jaxpr/jit(diagonal)/cond/branch_0_fun/gather | solution.py:52
  1225.3 5.5 fusion.46
  1242.4 16.9 %gather_fusion = f32[1024]{0:T(1024)S(1)} fusion(f32[1024,1024]{1,0:T(8,128)} %convolution_add_fusion.2, s32[1024]{0:T(1024)S(1)} %bitcast.73), kind=kCustom, calls=%fused_computation.clone.1 | custom fusion | bytes 16384 | tf_op jit(solution)/shard_map/while/body/eval_jaxpr/jit(diagonal)/cond/branch_0_fun/gather | solution.py:52
  1268.6 5.5 fusion.46
  1285.7 16.9 %gather_fusion = f32[1024]{0:T(1024)S(1)} fusion(f32[1024,1024]{1,0:T(8,128)} %convolution_add_fusion.2, s32[1024]{0:T(1024)S(1)} %bitcast.73), kind=kCustom, calls=%fused_computation.clone.1 | custom fusion | bytes 16384 | tf_op jit(solution)/shard_map/while/body/eval_jaxpr/jit(diagonal)/cond/branch_0_fun/gather | solution.py:52
  1311.9 5.5 fusion.46
  1329.0 16.9 %gather_fusion = f32[1024]{0:T(1024)S(1)} fusion(f32[1024,1024]{1,0:T(8,128)} %convolution_add_fusion.2, s32[1024]{0:T(1024)S(1)} %bitcast.73), kind=kCustom, calls=%fused_computation.clone.1 | custom fusion | bytes 16384 | tf_op jit(solution)/shard_map/while/body/eval_jaxpr/jit(diagonal)/cond/branch_0_fun/gather | solution.py:52
  1355.2 5.5 fusion.46
  1372.2 16.9 %gather_fusion = f32[1024]{0:T(1024)S(1)} fusion(f32[1024,1024]{1,0:T(8,128)} %convolution_add_fusion.2, s32[1024]{0:T(1024)S(1)} %bitcast.73), kind=kCustom, calls=%fused_computation.clone.1 | custom fusion | bytes 16384 | tf_op jit(solution)/shard_map/while/body/eval_jaxpr/jit(diagonal)/cond/branch_0_fun/gather | solution.py:52
  1398.4 5.5 fusion.46
  1415.5 16.9 %gather_fusion = f32[1024]{0:T(1024)S(1)} fusion(f32[1024,1024]{1,0:T(8,128)} %convolution_add_fusion.2, s32[1024]{0:T(1024)S(1)} %bitcast.73), kind=kCustom, calls=%fused_computation.clone.1 | custom fusion | bytes 16384 | tf_op jit(solution)/shard_map/while/body/eval_jaxpr/jit(diagonal)/cond/branch_0_fun/gather | solution.py:52
  1441.7 5.5 fusion.46
  (129 shorter events, 326.4 us)
Async XLA Ops:
  0.0 15.9 %copy-start.1 = (f32[8,1024]{1,0:T(8,128)S(1)}, f32[8,1024]{1,0:T(8,128)}, u32[]{:S(2)}) copy-start(f32[8,1024]{1,0:T(8,128)} %param.5) | copy-start | bytes 98308
  0.0 55.2 %slice-start = ((s8[16777216]{0:T(1024)(128)(4,1)}), s8[4194304]{0:T(1024)(128)(4,1)S(1)}, s32[]{:S(2)}) async-start(s8[16777216]{0:T(1024)(128)(4,1)} %bitcast.76), calls=%async_computation.2 | async-start | bytes 8388608
  0.0 55.2 %slice-start.1 = ((s8[16777216]{0:T(1024)(128)(4,1)}), s8[4194304]{0:T(1024)(128)(4,1)S(1)}, s32[]{:S(2)}) async-start(s8[16777216]{0:T(1024)(128)(4,1)} %bitcast.76), calls=%async_computation.3 | async-start | bytes 8388608
  0.0 55.2 %slice-start.2 = ((s8[16777216]{0:T(1024)(128)(4,1)}), s8[4194304]{0:T(1024)(128)(4,1)S(1)}, s32[]{:S(2)}) async-start(s8[16777216]{0:T(1024)(128)(4,1)} %bitcast.76), calls=%async_computation.4 | async-start | bytes 8388608
  10.3 44.9 %slice-start.3 = ((s8[16777216]{0:T(1024)(128)(4,1)}), s8[4194304]{0:T(1024)(128)(4,1)S(1)}, s32[]{:S(2)}) async-start(s8[16777216]{0:T(1024)(128)(4,1)} %bitcast.76), calls=%async_computation.5 | async-start | bytes 8388608
  10.5 44.5 %collective-permute-start = (bf16[128,7,1024]{2,0,1:T(8,128)(2,1)S(1)}, bf16[128,7,1024]{2,0,1:T(8,128)(2,1)S(1)}, u32[]{:S(2)}, u32[]{:S(2)}) collective-permute-start(bf16[128,7,1024]{2,0,1:T(8,128)(2,1)S(1)} %slice.74), channel_id=1, source_target_pairs={{0,1},{1,2},{2,3},{4,5},{5,6},{6,7},{8,9},{9,10},{10,11},{12,13},{... | collective-permute-start | bytes 5505032 | tf_op jit(solution)/shard_map/ppermute | solution.py:16
  57.7 6.8 copy-start
  372.7 370.5 %all-to-all-start.1 = ((bf16[128,1024,64]{1,2,0:T(8,128)(2,1)}), bf16[128,1024,64]{1,2,0:T(8,128)(2,1)}, u32[]{:S(2)}, u32[]{:S(2)}) async-start(bf16[128,1024,64]{1,2,0:T(8,128)(2,1)} %copy.40), calls=%async_computation.1 | async-start | bytes 33554432 | tf_op jit(solution)/shard_map/all_to_all | solution.py:65
where the time goes:
time: 1460 us; the launch traced here: 1450 us
  local copies, waits for them, and re-layouts  457 us (31%)
  waiting for transfers between devices  384 us (26%)
  matrix products  263 us (18%)
  blocking collectives  188 us (13%)
  other arithmetic  146 us (10%)
    all_to_all x1, waiting for transfers between devices, shards(): lax.all_to_all(lax.all_to_all(spectra, 'inp', split_axis=0, concat_axis=1...  363 us
    gather x16, local copies, waits for them, and re-layouts, correlate(): scales = lax.rsqrt(jnp.diagonal(real_gram) + 1e-06)  270 us
    all_to_all x1, blocking collectives, shards(): lax.all_to_all(spectra, 'inp', split_axis=0, concat_axis=1, tiled=True)  188 us
    another operation x16, other arithmetic, correlate(): jnp.stack([real_gram * outer, imag_gram * outer]).astype(jnp.bfloat16)  87.4 us
    dot_general x16, local copies, waits for them, and re-layouts, correlate(): lax.dot_general(imag_part, real_part, dims, preferred_element_type=jnp.fl...  86.1 us
    dot_general x16, matrix products, correlate(): lax.dot_general(imag_part, imag_part, dims, preferred_element_type=jnp.fl...  83.7 us
    dot_general x16, matrix products, correlate(): lax.dot_general(real_part, real_part, dims, preferred_element_type=jnp.fl...  62.6 us
    dot_general x16, matrix products, correlate(): lax.dot_general(imag_part, real_part, dims, preferred_element_type=jnp.fl...  62.4 us
  transfers between devices with their start and end apart: 2, of which 2 were waited for; matrix products, arithmetic and copies ran while one was open for 1% of the time, Pallas kernels for 0%

commit v1 on v0

v1 whole, which is shorter than its diff:
```python
import functools

import jax
import jax.numpy as jnp
import numpy as np
from jax import lax
from jax.experimental import pallas as pl
from jax.experimental.pallas import tpu as pltpu
from jax.sharding import PartitionSpec as P

LANES = 128
ROWS = 16
CHUNK = 4
VMEM = 56 * 1024 * 1024


def shifted(block, axis, distance):
    devices = range(lax.axis_size(axis))
    route = [(i - distance, i) for i in devices if i - distance in devices]
    return lax.ppermute(block, axis, route)


def dft_rows(frame, columns):
    sample = np.arange(frame, dtype=np.int64)[None, :]
    columns = columns[:, None]
    phase = (sample * (columns // 2) % frame) * (2.0 * np.pi / frame)
    table = np.where(columns % 2 == 0, np.cos(phase), -np.sin(phase))
    return jnp.asarray(table.astype(jnp.bfloat16))


def fir(load, store, coefficients, count):
    taps = len(coefficients)
    window = [load(f) for f in range(taps - 1)]
    for s in range(count):
        window.append(load(s + taps - 1))
        total = window[0] * coefficients[0]
        for k in range(1, taps):
            total = total + window[k] * coefficients[k]
        store(s, total)
        window.pop(0)


def main_filter_kernel(taps, frame, spectra, skip, v_ref, p_ref, o_ref):
    @pl.loop(0, frame // LANES)
    def _(block):
        at = pl.multiple_of(block * LANES, LANES)
        lanes = pl.ds(at, LANES)
        coefficients = [
            jnp.broadcast_to(p_ref[pl.ds(k, 1), lanes], (ROWS, LANES)) for k in range(taps)
        ]
        first = skip - taps + 1

        def load(f):
            return v_ref[:, pl.ds((first + f) * frame + at, LANES)].astype(jnp.float32)

        def store(s, value):
            o_ref[skip + s, :, lanes] = value.astype(jnp.bfloat16)

        fir(load, store, coefficients, spectra - skip)


def edge_filter_kernel(taps, frame, skip, v_ref, e_ref, p_ref, a_ref, o_ref):
    del a_ref

    @pl.loop(0, frame // LANES)
    def _(block):
        at = pl.multiple_of(block * LANES, LANES)
        lanes = pl.ds(at, LANES)
        coefficients = [
            jnp.broadcast_to(p_ref[pl.ds(k, 1), lanes], (ROWS, LANES)) for k in range(taps)
        ]

        def load(f):
            if f < taps - 1:
                return e_ref[:, pl.ds(f * frame + at, LANES)].astype(jnp.float32)
            return v_ref[:, pl.ds((f - taps + 1) * frame + at, LANES)].astype(jnp.float32)

        def store(s, value):
            o_ref[s, :, lanes] = value.astype(jnp.bfloat16)

        fir(load, store, coefficients, skip)


def filter_frames(voltages, earlier, prototype):
    inputs, samples = voltages.shape
    taps, frame = prototype.shape
    spectra = samples // frame
    skip = 8
    assert taps - 1 <= skip < spectra
    params = pltpu.CompilerParams(vmem_limit_bytes=VMEM)
    shape = jax.ShapeDtypeStruct((spectra, inputs, frame), jnp.bfloat16)
    partial = pl.pallas_call(
        functools.partial(main_filter_kernel, taps, frame, spectra, skip),
        grid=(inputs // ROWS,),
        in_specs=[
            pl.BlockSpec((ROWS, samples), lambda r: (r, 0)),
            pl.BlockSpec((taps, frame), lambda r: (0, 0)),
        ],
        out_specs=pl.BlockSpec((spectra, ROWS, frame), lambda r: (0, r, 0)),
        out_shape=shape,
        compiler_params=params,
        cost_estimate=pl.CostEstimate(
            flops=2 * taps * inputs * samples,
            bytes_accessed=4 * inputs * samples,
            transcendentals=0,
        ),
        name="filter_main",
    )(voltages, prototype)
    return pl.pallas_call(
        functools.partial(edge_filter_kernel, taps, frame, skip),
        grid=(inputs // ROWS,),
        in_specs=[
            pl.BlockSpec((ROWS, skip * frame), lambda r: (r, 0)),
            pl.BlockSpec((ROWS, (taps - 1) * frame), lambda r: (r, 0)),
            pl.BlockSpec((taps, frame), lambda r: (0, 0)),
            pl.BlockSpec(memory_space=pl.ANY),
        ],
        out_specs=pl.BlockSpec((skip, ROWS, frame), lambda r: (0, r, 0)),
        out_shape=shape,
        input_output_aliases={3: 0},
        compiler_params=params,
        cost_estimate=pl.CostEstimate(
            flops=2 * taps * inputs * skip * frame,
            bytes_accessed=6 * inputs * skip * frame,
            transcendentals=0,
        ),
        name="filter_edge",
    )(voltages, earlier, prototype, partial)


def dft_kernel(columns, inputs, t_ref, f_ref, o_ref, turn):
    group = max(1, 256 // inputs)
    for s in range(0, ROWS, group):
        frames = f_ref[pl.ds(s, group)].reshape(group * inputs, f_ref.shape[2])
        product = lax.dot_general(
            t_ref[...], frames, (((1,), (1,)), ((), ())), preferred_element_type=jnp.float32
        )
        for part in range(group):
            turn[pl.ds(s + part, columns, stride=ROWS), :] = product[
                :, part * inputs : (part + 1) * inputs
            ]
    o_ref[...] = turn[...].reshape(columns, ROWS, inputs).astype(jnp.bfloat16)


def transform(table, filtered):
    spectra, inputs, frame = filtered.shape
    columns = table.shape[0]
    if inputs % LANES:
        dims = (((1,), (2,)), ((), ()))
        out = lax.dot_general(table, filtered, dims, preferred_element_type=jnp.float32)
        return out.astype(jnp.bfloat16)
    return pl.pallas_call(
        functools.partial(dft_kernel, columns, inputs),
        grid=(spectra // ROWS,),
        in_specs=[
            pl.BlockSpec((columns, frame), lambda b: (0, 0)),
            pl.BlockSpec((ROWS, inputs, frame), lambda b: (b, 0, 0)),
        ],
        out_specs=pl.BlockSpec((columns, ROWS, inputs), lambda b: (0, b, 0)),
        out_shape=jax.ShapeDtypeStruct((columns, spectra, inputs), jnp.bfloat16),
        scratch_shapes=[pltpu.VMEM((columns * ROWS, inputs), jnp.float32)],
        compiler_params=pltpu.CompilerParams(vmem_limit_bytes=VMEM),
        cost_estimate=pl.CostEstimate(
            flops=2 * columns * spectra * inputs * frame,
            bytes_accessed=2 * spectra * inputs * (frame + columns),
            transcendentals=0,
        ),
        name="dft",
    )(table, filtered)


def correlate_kernel(block, *refs):
    r_ref, o_ref, right, left = refs[0], refs[-3], refs[-2], refs[-1]
    groups, slabs, _, _, here, width = r_ref.shape
    spectra = slabs * here
    inputs = groups * width
    for part in range(2):
        for t in range(slabs):
            for g in range(groups):
                right[
                    pl.ds(part * spectra + t * here, here), pl.ds(g * width, width)
                ] = r_ref[g, t, 0, part]
    power = jnp.zeros((1, inputs), jnp.float32)
    for at in range(0, 2 * spectra, ROWS):
        piece = right[pl.ds(at, ROWS), :].astype(jnp.float32)
        power = power + jnp.sum(piece * piece, axis=0, keepdims=True)
    across = lax.rsqrt(power + 1e-06)
    left[...] = right[...].T

    @pl.loop(0, inputs // block)
    def _(index):
        rows = pl.ds(pl.multiple_of(index * block, block), block)
        own = left[rows, :]
        wide = own.astype(jnp.float32)
        down = lax.rsqrt(jnp.sum(wide * wide, axis=1, keepdims=True) + 1e-06)
        swapped = jnp.concatenate([own[:, spectra:], -own[:, :spectra]], axis=1)
        for part, operand in enumerate((own, swapped)):
            gram = jnp.dot(operand, right[...], preferred_element_type=jnp.float32)
            o_ref[0, part, rows, :] = (gram * down * across).astype(jnp.bfloat16)


def correlate(pieces, total, first, channels):
    groups, slabs, chunk, _, here, width = pieces.shape
    if width % LANES:
        pieces = pieces.transpose(2, 3, 1, 4, 0, 5)
        pieces = pieces.reshape(1, 1, chunk, 2, slabs * here, groups * width)
        groups, slabs, chunk, _, here, width = pieces.shape
    inputs, spectra = groups * width, slabs * here
    in_specs = [pl.BlockSpec((groups, slabs, 1, 2, here, width), lambda c: (0, 0, c, 0, 0, 0))]
    operands = [pieces]
    aliases = {}
    if total is not None:
        in_specs.append(pl.BlockSpec(memory_space=pl.ANY))
        operands.append(total)
        aliases = {1: 0}
    return pl.pallas_call(
        functools.partial(correlate_kernel, min(256, inputs)),
        grid=(chunk,),
        in_specs=in_specs,
        out_specs=pl.BlockSpec((1, 2, inputs, inputs), lambda c: (first + c, 0, 0, 0)),
        out_shape=jax.ShapeDtypeStruct((channels, 2, inputs, inputs), jnp.bfloat16),
        input_output_aliases=aliases,
        scratch_shapes=[
            pltpu.VMEM((2 * spectra, inputs), jnp.bfloat16),
            pltpu.VMEM((inputs, 2 * spectra), jnp.bfloat16),
        ],
        compiler_params=pltpu.CompilerParams(vmem_limit_bytes=VMEM),
        cost_estimate=pl.CostEstimate(
            flops=8 * chunk * inputs * inputs * spectra,
            bytes_accessed=4 * chunk * inputs * (inputs + spectra),
            transcendentals=0,
        ),
        name="correlate",
    )(*operands)


def shards(voltages, prototype):
    inputs, samples = voltages.shape
    taps, frame = prototype.shape
    spectra = samples // frame
    groups = lax.axis_size("inp")
    slabs = lax.axis_size("tm")
    devices = groups * slabs
    channels = frame // 2 // devices
    chunk = min(CHUNK, channels)
    earlier = shifted(voltages[:, (spectra - taps + 1) * frame :], "tm", 1)
    filtered = filter_frames(voltages, earlier, prototype)
    device = np.arange(devices)[:, None, None]
    total = None
    for first in range(0, channels, chunk):
        channel = device * channels + first + np.arange(chunk)[None, :, None]
        columns = (2 * channel + np.arange(2)[None, None, :]).reshape(-1)
        spectrum = transform(dft_rows(frame, columns), filtered)
        spectrum = spectrum.reshape(devices, 2 * chunk, spectra, inputs)
        turned = lax.all_to_all(
            spectrum, ("inp", "tm"), split_axis=0, concat_axis=0, tiled=True
        )
        pieces = turned.reshape(groups, slabs, chunk, 2, spectra, inputs)
        total = correlate(pieces, total, first, channels)
    return total


def solution(mesh):
    return jax.shard_map(
        shards,
        mesh=mesh,
        in_specs=(P("inp", "tm"), P()),
        out_specs=P(("inp", "tm"), None, None, None),
        check_vma=False,
    )
```

time: 1460 us -> 478 us (0.33)
  local copies, waits for them, and re-layouts: 457 us -> 2.86 us
  matrix products: 263 us -> 0 us
  blocking collectives: 188 us -> 0 us
  other arithmetic: 146 us -> 0 us
  Pallas kernels: 0 us -> 143 us
  waiting for transfers between devices: 384 us -> 301 us
  starting transfers between devices: 12.5 us -> 29.2 us
    gather x16 -> x0, local copies, waits for them, and re-layouts: 270 us -> none  [correlate(): scales = lax.rsqrt(jnp.diagonal(real_gram) + 1e-06)]
    dot_general x49 -> x0, matrix products: 263 us -> none  [the longest x16 83.7 us: correlate(): lax.dot_general(imag_part, imag_part, dims, preferred_element_type=jnp.fl...]
    all_to_all x1 -> x0, blocking collectives: 188 us -> none  [shards(): lax.all_to_all(spectra, 'inp', split_axis=0, concat_axis=1, tiled=True)]
    pallas_call x0 -> x10, Pallas kernels: none -> 143 us  [the longest x4 69.9 us: correlate(): pl.pallas_call(functools.partial(correlate_kernel, min(256, inputs)), gri...]
    another operation x16 -> x0, other arithmetic: 87.4 us -> none  [correlate(): jnp.stack([real_gram * outer, imag_gram * outer]).astype(jnp.bfloat16)]
    dot_general x16 -> x0, local copies, waits for them, and re-layouts: 86.1 us -> none  [correlate(): lax.dot_general(imag_part, real_part, dims, preferred_element_type=jnp.fl...]
    all_to_all x1 -> x4, waiting for transfers between devices: 363 us -> 283 us  [shards(): lax.all_to_all(spectrum, ('inp', 'tm'), split_axis=0, concat_axis=0, tile...]
    all_to_all x3 -> x0, local copies, waits for them, and re-layouts: 65.7 us -> none  [the longest x2 51.7 us: shards(): lax.all_to_all(spectra, 'inp', split_axis=0, concat_axis=1, tiled=True)]
  transfers between devices with their start and end apart: 2 -> 5, of which waited for: 2 -> 5; matrix products, arithmetic and copies ran while one was open for 1% -> 0% of each run, Pallas kernels for 0% -> 22%
where the time goes in v1:
time: 478 us; the launch traced here: 476 us
  waiting for transfers between devices  301 us (63%)
  Pallas kernels  143 us (30%)
  starting transfers between devices  29.2 us (6%)
    all_to_all x4, waiting for transfers between devices, shards(): lax.all_to_all(spectrum, ('inp', 'tm'), split_axis=0, concat_axis=0, tile...  283 us
    pallas_call x4, Pallas kernels, correlate(): pl.pallas_call(functools.partial(correlate_kernel, min(256, inputs)), gri...  69.9 us
    pallas_call x4, Pallas kernels, transform(): pl.pallas_call(functools.partial(dft_kernel, columns, inputs), grid=(spec...  44.7 us
    all_to_all x4, starting transfers between devices, shards(): lax.all_to_all(spectrum, ('inp', 'tm'), split_axis=0, concat_axis=0, tile...  24.2 us
    pallas_call x1, Pallas kernels, filter_frames(): pl.pallas_call(functools.partial(main_filter_kernel, taps, frame, spectra...  20.7 us
    ppermute x1, waiting for transfers between devices, shifted(): return lax.ppermute(block, axis, route)  18.4 us
  transfers between devices with their start and end apart: 5, of which 5 were waited for; matrix products, arithmetic and copies ran while one was open for 0% of the time, Pallas kernels for 22%

profile of v1, /device:TPU:0, one launch (start us, length us, event | category | flops | bytes accessed | tf_op | source)
XLA Modules:
  0.0 476.0 jit_solution(5622834902442267508)
XLA Ops:
  0.0 1.6 slice.3
  1.6 5.0 %collective-permute-start = (bf16[128,7168]{1,0:T(8,128)(2,1)S(1)}, bf16[128,7168]{1,0:T(8,128)(2,1)S(1)}, u32[]{:S(2)}, u32[]{:S(2)}) collective-permute-start(bf16[128,7168]{1,0:T(8,128)(2,1)S(1)} %slice.3), channel_id=1, source_target_pairs={{0,1},{1,2},{2,3},{4,5},{5,6},{6,7},{8,9},{9,10},{10,11},{12,13},{... | collective-permute-start | bytes 5505032 | tf_op jit(solution)/shard_map/ppermute | solution.py:20
  6.7 20.7 %filter_main.1.a_ref = bf16[64,128,1024]{2,1,0:T(8,128)(2,1)} custom-call(bf16[128,65536]{1,0:T(8,128)(2,1)} %v_ref.3, f32[8,1024]{1,0:T(8,128)} %p_ref.3), custom_call_target="tpu_custom_call" | custom-call | flops 134217728 | bytes 33554432 | tf_op jit(solution)/shard_map/filter_main/pallas_call | solution.py:92
  27.4 18.4 %collective-permute-done.e_ref = bf16[128,7168]{1,0:T(8,128)(2,1)S(1)} collective-permute-done((bf16[128,7168]{1,0:T(8,128)(2,1)S(1)}, bf16[128,7168]{1,0:T(8,128)(2,1)S(1)}, u32[]{:S(2)}, u32[]{:S(2)}) %collective-permute-start) | collective-permute-done | bytes 1835040 | tf_op jit(solution)/shard_map/ppermute | solution.py:20
  45.8 0.0 copy-start
  45.8 1.2 copy-done
  47.1 7.4 %filter_edge.1.f_ref = bf16[64,128,1024]{2,1,0:T(8,128)(2,1)} custom-call(bf16[128,65536]{1,0:T(8,128)(2,1)} %v_ref.3, bf16[128,7168]{1,0:T(8,128)(2,1)} %copy-done, f32[8,1024]{1,0:T(8,128)} %p_ref.3, bf16[64,128,1024]{2,1,0:T(8,128)(2,1)} %filter_main.1.a_ref), custom_call_target="tpu_custom_call", output_to_operand_aliasing={{}: (3, {})} | custom-call | flops 16777216 | bytes 6291456 | tf_op jit(solution)/shard_map/filter_edge/pallas_call | solution.py:109
  54.4 11.2 %dft.7 = bf16[256,64,128]{2,1,0:T(8,128)(2,1)} custom-call(bf16[256,1024]{1,0:T(8,128)(2,1)} %constant.8.clone.t_ref, bf16[64,128,1024]{2,1,0:T(8,128)(2,1)} %filter_edge.1.f_ref), custom_call_target="tpu_custom_call" | custom-call | flops 4294967296 | bytes 20971520 | tf_op jit(solution)/shard_map/dft/pallas_call | solution.py:152
  65.6 6.9 %all-to-all-start.3 = ((bf16[32,8,64,128]{3,2,1,0:T(8,128)(2,1)}), bf16[32,8,64,128]{3,2,1,0:T(8,128)(2,1)}, u32[]{:S(2)}, u32[]{:S(2)}) async-start(bf16[32,8,64,128]{3,2,1,0:T(8,128)(2,1)} %bitcast.11), calls=%async_computation.3 | async-start | bytes 8388608 | tf_op jit(solution)/shard_map/all_to_all | solution.py:255
  72.5 11.1 %dft.6 = bf16[256,64,128]{2,1,0:T(8,128)(2,1)} custom-call(bf16[256,1024]{1,0:T(8,128)(2,1)} %constant.9.clone.t_ref, bf16[64,128,1024]{2,1,0:T(8,128)(2,1)} %filter_edge.1.f_ref), custom_call_target="tpu_custom_call" | custom-call | flops 4294967296 | bytes 20971520 | tf_op jit(solution)/shard_map/dft/pallas_call | solution.py:152
  83.7 81.1 %all-to-all-done.3 = bf16[32,8,64,128]{3,2,1,0:T(8,128)(2,1)} async-done(((bf16[32,8,64,128]{3,2,1,0:T(8,128)(2,1)}), bf16[32,8,64,128]{3,2,1,0:T(8,128)(2,1)}, u32[]{:S(2)}, u32[]{:S(2)}) %all-to-all-start.3) | async-done | bytes 4194336 | tf_op jit(solution)/shard_map/all_to_all | solution.py:255
  164.8 5.7 %all-to-all-start.2 = ((bf16[32,8,64,128]{3,2,1,0:T(8,128)(2,1)}), bf16[32,8,64,128]{3,2,1,0:T(8,128)(2,1)}, u32[]{:S(2)}, u32[]{:S(2)}) async-start(bf16[32,8,64,128]{3,2,1,0:T(8,128)(2,1)} %bitcast.10), calls=%async_computation.2 | async-start | bytes 8388608 | tf_op jit(solution)/shard_map/all_to_all | solution.py:255
  170.5 11.2 %dft.5 = bf16[256,64,128]{2,1,0:T(8,128)(2,1)} custom-call(bf16[256,1024]{1,0:T(8,128)(2,1)} %constant.10.clone.t_ref, bf16[64,128,1024]{2,1,0:T(8,128)(2,1)} %filter_edge.1.f_ref), custom_call_target="tpu_custom_call" | custom-call | flops 4294967296 | bytes 20971520 | tf_op jit(solution)/shard_map/dft/pallas_call | solution.py:152
  181.6 81.0 %all-to-all-done.2 = bf16[32,8,64,128]{3,2,1,0:T(8,128)(2,1)} async-done(((bf16[32,8,64,128]{3,2,1,0:T(8,128)(2,1)}), bf16[32,8,64,128]{3,2,1,0:T(8,128)(2,1)}, u32[]{:S(2)}, u32[]{:S(2)}) %all-to-all-start.2) | async-done | bytes 4194336 | tf_op jit(solution)/shard_map/all_to_all | solution.py:255
  262.7 5.7 %all-to-all-start.1 = ((bf16[32,8,64,128]{3,2,1,0:T(8,128)(2,1)}), bf16[32,8,64,128]{3,2,1,0:T(8,128)(2,1)}, u32[]{:S(2)}, u32[]{:S(2)}) async-start(bf16[32,8,64,128]{3,2,1,0:T(8,128)(2,1)} %bitcast.9), calls=%async_computation.1 | async-start | bytes 8388608 | tf_op jit(solution)/shard_map/all_to_all | solution.py:255
  268.4 11.1 %dft.4 = bf16[256,64,128]{2,1,0:T(8,128)(2,1)} custom-call(bf16[256,1024]{1,0:T(8,128)(2,1)} %constant.11.clone.t_ref, bf16[64,128,1024]{2,1,0:T(8,128)(2,1)} %filter_edge.1.f_ref), custom_call_target="tpu_custom_call" | custom-call | flops 4294967296 | bytes 20971520 | tf_op jit(solution)/shard_map/dft/pallas_call | solution.py:152
  279.5 81.1 %all-to-all-done.1 = bf16[32,8,64,128]{3,2,1,0:T(8,128)(2,1)} async-done(((bf16[32,8,64,128]{3,2,1,0:T(8,128)(2,1)}), bf16[32,8,64,128]{3,2,1,0:T(8,128)(2,1)}, u32[]{:S(2)}, u32[]{:S(2)}) %all-to-all-start.1) | async-done | bytes 4194336 | tf_op jit(solution)/shard_map/all_to_all | solution.py:255
  360.6 5.9 %all-to-all-start = ((bf16[32,8,64,128]{3,2,1,0:T(8,128)(2,1)}), bf16[32,8,64,128]{3,2,1,0:T(8,128)(2,1)}, u32[]{:S(2)}, u32[]{:S(2)}) async-start(bf16[32,8,64,128]{3,2,1,0:T(8,128)(2,1)} %bitcast.8), calls=%async_computation | async-start | bytes 8388608 | tf_op jit(solution)/shard_map/all_to_all | solution.py:255
  366.5 17.5 %correlate.4.refs_1_ = bf16[16,2,1024,1024]{3,2,1,0:T(8,128)(2,1)} custom-call(bf16[8,4,4,2,64,128]{5,4,3,2,1,0:T(8,128)(2,1)} %bitcast.7.refs_0_), custom_call_target="tpu_custom_call" | custom-call | flops 8589934592 | bytes 20971520 | tf_op jit(solution)/shard_map/correlate/pallas_call | solution.py:216
  384.0 17.5 %correlate.5.refs_1_ = bf16[16,2,1024,1024]{3,2,1,0:T(8,128)(2,1)} custom-call(bf16[8,4,4,2,64,128]{5,4,3,2,1,0:T(8,128)(2,1)} %bitcast.5.refs_0_, bf16[16,2,1024,1024]{3,2,1,0:T(8,128)(2,1)} %correlate.4.refs_1_), custom_call_target="tpu_custom_call", output_to_operand_aliasing={{}: (1, {})} | custom-call | flops 8589934592 | bytes 20971520 | tf_op jit(solution)/shard_map/correlate/pallas_call | solution.py:216
  401.4 17.5 %correlate.6.refs_1_ = bf16[16,2,1024,1024]{3,2,1,0:T(8,128)(2,1)} custom-call(bf16[8,4,4,2,64,128]{5,4,3,2,1,0:T(8,128)(2,1)} %bitcast.3.refs_0_, bf16[16,2,1024,1024]{3,2,1,0:T(8,128)(2,1)} %correlate.5.refs_1_), custom_call_target="tpu_custom_call", output_to_operand_aliasing={{}: (1, {})} | custom-call | flops 8589934592 | bytes 20971520 | tf_op jit(solution)/shard_map/correlate/pallas_call | solution.py:216
  418.9 39.6 %all-to-all-done = bf16[32,8,64,128]{3,2,1,0:T(8,128)(2,1)} async-done(((bf16[32,8,64,128]{3,2,1,0:T(8,128)(2,1)}), bf16[32,8,64,128]{3,2,1,0:T(8,128)(2,1)}, u32[]{:S(2)}, u32[]{:S(2)}) %all-to-all-start) | async-done | bytes 4194336 | tf_op jit(solution)/shard_map/all_to_all | solution.py:255
  458.5 17.5 %correlate.7 = bf16[16,2,1024,1024]{3,2,1,0:T(8,128)(2,1)} custom-call(bf16[8,4,4,2,64,128]{5,4,3,2,1,0:T(8,128)(2,1)} %bitcast.1.refs_0_, bf16[16,2,1024,1024]{3,2,1,0:T(8,128)(2,1)} %correlate.6.refs_1_), custom_call_target="tpu_custom_call", output_to_operand_aliasing={{}: (1, {})} | custom-call | flops 8589934592 | bytes 20971520 | tf_op jit(solution)/shard_map/correlate/pallas_call | solution.py:216
Async XLA Ops:
  1.6 44.2 %collective-permute-start = (bf16[128,7168]{1,0:T(8,128)(2,1)S(1)}, bf16[128,7168]{1,0:T(8,128)(2,1)S(1)}, u32[]{:S(2)}, u32[]{:S(2)}) collective-permute-start(bf16[128,7168]{1,0:T(8,128)(2,1)S(1)} %slice.3), channel_id=1, source_target_pairs={{0,1},{1,2},{2,3},{4,5},{5,6},{6,7},{8,9},{9,10},{10,11},{12,13},{... | collective-permute-start | bytes 5505032 | tf_op jit(solution)/shard_map/ppermute | solution.py:20
  45.8 1.2 copy-start
  65.6 99.1 %all-to-all-start.3 = ((bf16[32,8,64,128]{3,2,1,0:T(8,128)(2,1)}), bf16[32,8,64,128]{3,2,1,0:T(8,128)(2,1)}, u32[]{:S(2)}, u32[]{:S(2)}) async-start(bf16[32,8,64,128]{3,2,1,0:T(8,128)(2,1)} %bitcast.11), calls=%async_computation.3 | async-start | bytes 8388608 | tf_op jit(solution)/shard_map/all_to_all | solution.py:255
  164.8 97.9 %all-to-all-start.2 = ((bf16[32,8,64,128]{3,2,1,0:T(8,128)(2,1)}), bf16[32,8,64,128]{3,2,1,0:T(8,128)(2,1)}, u32[]{:S(2)}, u32[]{:S(2)}) async-start(bf16[32,8,64,128]{3,2,1,0:T(8,128)(2,1)} %bitcast.10), calls=%async_computation.2 | async-start | bytes 8388608 | tf_op jit(solution)/shard_map/all_to_all | solution.py:255
  262.7 97.9 %all-to-all-start.1 = ((bf16[32,8,64,128]{3,2,1,0:T(8,128)(2,1)}), bf16[32,8,64,128]{3,2,1,0:T(8,128)(2,1)}, u32[]{:S(2)}, u32[]{:S(2)}) async-start(bf16[32,8,64,128]{3,2,1,0:T(8,128)(2,1)} %bitcast.9), calls=%async_computation.1 | async-start | bytes 8388608 | tf_op jit(solution)/shard_map/all_to_all | solution.py:255
  360.6 97.9 %all-to-all-start = ((bf16[32,8,64,128]{3,2,1,0:T(8,128)(2,1)}), bf16[32,8,64,128]{3,2,1,0:T(8,128)(2,1)}, u32[]{:S(2)}, u32[]{:S(2)}) async-start(bf16[32,8,64,128]{3,2,1,0:T(8,128)(2,1)} %bitcast.8), calls=%async_computation | async-start | bytes 8388608 | tf_op jit(solution)/shard_map/all_to_all | solution.py:255

commit v2 on v1

v2 whole, which is shorter than its diff:
```python
import functools

import jax
import jax.numpy as jnp
import numpy as np
from jax import lax
from jax.experimental import pallas as pl
from jax.experimental.pallas import tpu as pltpu
from jax.sharding import PartitionSpec as P

LANES = 128
ROWS = 16
VMEM = 63 * 1024 * 1024
WEIGHT = 8


def shifted(block, axis, distance):
    devices = range(lax.axis_size(axis))
    route = [(i - distance, i) for i in devices if i - distance in devices]
    return lax.ppermute(block, axis, route)


def dft_rows(frame, columns):
    sample = np.arange(frame, dtype=np.int64)[None, :]
    columns = columns[:, None]
    phase = (sample * (columns // 2) % frame) * (2.0 * np.pi / frame)
    table = np.where(columns % 2 == 0, np.cos(phase), -np.sin(phase))
    return jnp.asarray(table.astype(jnp.bfloat16))


def fir(load, store, coefficients, count):
    taps = len(coefficients)
    window = [load(f) for f in range(taps - 1)]
    for s in range(count):
        window.append(load(s + taps - 1))
        total = window[0] * coefficients[0]
        for k in range(1, taps):
            total = total + window[k] * coefficients[k]
        store(s, total)
        window.pop(0)


def main_filter_kernel(taps, frame, spectra, skip, v_ref, p_ref, o_ref):
    @pl.loop(0, frame // LANES)
    def _(block):
        at = pl.multiple_of(block * LANES, LANES)
        lanes = pl.ds(at, LANES)
        coefficients = [
            jnp.broadcast_to(p_ref[pl.ds(k, 1), lanes], (ROWS, LANES)) for k in range(taps)
        ]
        first = skip - taps + 1

        def load(f):
            return v_ref[:, pl.ds((first + f) * frame + at, LANES)].astype(jnp.float32)

        def store(s, value):
            o_ref[s, :, lanes] = value.astype(jnp.bfloat16)

        fir(load, store, coefficients, spectra - skip)


def edge_filter_kernel(taps, frame, skip, v_ref, e_ref, p_ref, o_ref):
    @pl.loop(0, frame // LANES)
    def _(block):
        at = pl.multiple_of(block * LANES, LANES)
        lanes = pl.ds(at, LANES)
        coefficients = [
            jnp.broadcast_to(p_ref[pl.ds(k, 1), lanes], (ROWS, LANES)) for k in range(taps)
        ]

        def load(f):
            if f < taps - 1:
                return e_ref[:, pl.ds(f * frame + at, LANES)].astype(jnp.float32)
            return v_ref[:, pl.ds((f - taps + 1) * frame + at, LANES)].astype(jnp.float32)

        def store(s, value):
            o_ref[s, :, lanes] = value.astype(jnp.bfloat16)

        fir(load, store, coefficients, skip)


def filter_main(voltages, prototype):
    inputs, samples = voltages.shape
    taps, frame = prototype.shape
    spectra = samples // frame
    assert taps - 1 <= ROWS < spectra
    return pl.pallas_call(
        functools.partial(main_filter_kernel, taps, frame, spectra, ROWS),
        grid=(inputs // ROWS,),
        in_specs=[
            pl.BlockSpec((ROWS, samples), lambda r: (r, 0)),
            pl.BlockSpec((taps, frame), lambda r: (0, 0)),
        ],
        out_specs=pl.BlockSpec((spectra - ROWS, ROWS, frame), lambda r: (0, r, 0)),
        out_shape=jax.ShapeDtypeStruct((spectra - ROWS, inputs, frame), jnp.bfloat16),
        compiler_params=pltpu.CompilerParams(vmem_limit_bytes=VMEM),
        cost_estimate=pl.CostEstimate(
            flops=2 * taps * inputs * samples,
            bytes_accessed=4 * inputs * samples,
            transcendentals=0,
        ),
        name="filter_main",
    )(voltages, prototype)


def filter_edge(voltages, earlier, prototype):
    inputs = voltages.shape[0]
    taps, frame = prototype.shape
    return pl.pallas_call(
        functools.partial(edge_filter_kernel, taps, frame, ROWS),
        grid=(inputs // ROWS,),
        in_specs=[
            pl.BlockSpec((ROWS, ROWS * frame), lambda r: (r, 0)),
            pl.BlockSpec((ROWS, (taps - 1) * frame), lambda r: (r, 0)),
            pl.BlockSpec((taps, frame), lambda r: (0, 0)),
        ],
        out_specs=pl.BlockSpec((ROWS, ROWS, frame), lambda r: (0, r, 0)),
        out_shape=jax.ShapeDtypeStruct((ROWS, inputs, frame), jnp.bfloat16),
        compiler_params=pltpu.CompilerParams(vmem_limit_bytes=VMEM),
        cost_estimate=pl.CostEstimate(
            flops=512 * WEIGHT * taps * inputs * ROWS * frame,
            bytes_accessed=6 * inputs * ROWS * frame,
            transcendentals=0,
        ),
        name="filter_edge",
    )(voltages, earlier, prototype)


def dft_kernel(inputs, t_ref, f_ref, *refs):
    o_ref, turn = refs[-2], refs[-1]
    columns = t_ref.shape[0]
    group = max(1, 256 // inputs)
    for s in range(0, ROWS, group):
        frames = f_ref[pl.ds(s, group)].reshape(group * inputs, f_ref.shape[2])
        product = lax.dot_general(
            t_ref[...], frames, (((1,), (1,)), ((), ())), preferred_element_type=jnp.float32
        )
        for part in range(group):
            turn[pl.ds(s + part, columns, stride=ROWS), :] = product[
                :, part * inputs : (part + 1) * inputs
            ]
    o_ref[...] = turn[...].reshape(o_ref.shape).astype(jnp.bfloat16)


def transform(table, filtered, devices, rows, first, buffer):
    spectra, inputs, frame = filtered.shape
    columns = table.shape[0]
    height = columns // devices * ROWS
    assert first % height == 0
    split = 1
    while columns // split > 320 and devices % (2 * split) == 0:
        split *= 2
    in_specs = [
        pl.BlockSpec((columns // split, frame), lambda b, d: (d, 0)),
        pl.BlockSpec((ROWS, inputs, frame), lambda b, d: (b, 0, 0)),
    ]
    operands = [table, filtered]
    if buffer is not None:
        in_specs.append(pl.BlockSpec(memory_space=pl.ANY))
        operands.append(buffer)
    return pl.pallas_call(
        functools.partial(dft_kernel, inputs),
        grid=(spectra // ROWS, split),
        in_specs=in_specs,
        out_specs=pl.BlockSpec(
            (devices // split, height, inputs), lambda b, d: (d, first // height + b, 0)
        ),
        out_shape=jax.ShapeDtypeStruct((devices, rows, inputs), jnp.bfloat16),
        input_output_aliases={} if buffer is None else {2: 0},
        scratch_shapes=[pltpu.VMEM((columns // split * ROWS, inputs), jnp.float32)],
        compiler_params=pltpu.CompilerParams(vmem_limit_bytes=VMEM),
        cost_estimate=pl.CostEstimate(
            flops=WEIGHT * columns * spectra * inputs * frame,
            bytes_accessed=2 * spectra * inputs * (frame + columns),
            transcendentals=0,
        ),
        name="dft",
    )(*operands)


def correlate_block(block, o_ref, right, left):
    depth, inputs = right.shape
    spectra = depth // 2
    power = jnp.zeros((ROWS, inputs), jnp.float32)
    for at in range(0, depth, ROWS):
        piece = right[pl.ds(at, ROWS), :].astype(jnp.float32)
        power = power + piece * piece
    across = lax.rsqrt(jnp.sum(power, axis=0, keepdims=True) + 1e-06)
    down = jnp.broadcast_to(across, (8, inputs)).T[:, :1]
    left[...] = right[...].T
    for at in range(0, inputs, block):
        rows = pl.ds(at, block)
        own = left[rows, :]
        swapped = jnp.concatenate([own[:, spectra:], -own[:, :spectra]], axis=1)
        for part, operand in enumerate((own, swapped)):
            gram = jnp.dot(operand, right[...], preferred_element_type=jnp.float32)
            o_ref[0, part, rows, :] = (gram * down[at : at + block] * across).astype(jnp.bfloat16)


def correlate_kernel(block, slabs, count, *refs):
    blocks, o_ref, right, left = refs[:count], refs[-3], refs[-2], refs[-1]
    devices, _, width = blocks[0].shape
    spectra = right.shape[0] // 2
    for part in range(2):
        for device in range(devices):
            g, t = device // slabs, device % slabs
            for b, ref in enumerate(blocks):
                at = part * spectra + (t * len(blocks) + b) * ROWS
                right[pl.ds(at, ROWS), pl.ds(g * width, width)] = ref[
                    device, pl.ds(part * ROWS, ROWS), :
                ]
    correlate_block(block, o_ref, right, left)


def plain_correlate_kernel(block, r_ref, o_ref, right, left):
    right[...] = r_ref[0]
    correlate_block(block, o_ref, right, left)


def correlate(kernel, in_specs, operands, total, first, count, out_shape, spectra):
    inputs = out_shape.shape[-1]
    aliases = {}
    if total is not None:
        aliases = {len(operands): 0}
        in_specs = [*in_specs, pl.BlockSpec(memory_space=pl.ANY)]
        operands = [*operands, total]
    return pl.pallas_call(
        kernel,
        grid=(count,),
        in_specs=in_specs,
        out_specs=pl.BlockSpec((1, 2, inputs, inputs), lambda c: (first + c, 0, 0, 0)),
        out_shape=out_shape,
        input_output_aliases=aliases,
        scratch_shapes=[
            pltpu.VMEM((2 * spectra, inputs), jnp.bfloat16),
            pltpu.VMEM((inputs, 2 * spectra), jnp.bfloat16),
        ],
        compiler_params=pltpu.CompilerParams(vmem_limit_bytes=VMEM),
        cost_estimate=pl.CostEstimate(
            flops=8 * count * inputs * inputs * spectra,
            bytes_accessed=4 * count * inputs * (inputs + spectra),
            transcendentals=0,
        ),
        name="correlate",
    )(*operands)


def table_of(frame, devices, channels, first, count):
    channel = np.arange(devices)[:, None, None] * channels + first
    channel = channel + np.arange(count)[None, :, None]
    return dft_rows(frame, (2 * channel + np.arange(2)[None, None, :]).reshape(-1))


def exchange(rows):
    return lax.all_to_all(rows, ("inp", "tm"), split_axis=0, concat_axis=0, tiled=True)


def narrow(voltages, prototype, earlier, out_shape):
    inputs, samples = voltages.shape
    frame = prototype.shape[1]
    groups, slabs = lax.axis_size("inp"), lax.axis_size("tm")
    devices, channels = groups * slabs, out_shape.shape[0]
    spectra = samples // frame
    filtered = jnp.concatenate(
        [filter_edge(voltages, earlier, prototype), filter_main(voltages, prototype)]
    )
    table = table_of(frame, devices, channels, 0, channels)
    dims = (((1,), (2,)), ((), ()))
    rows = lax.dot_general(table, filtered, dims, preferred_element_type=jnp.float32)
    rows = rows.astype(jnp.bfloat16).reshape(devices, -1, inputs)
    turned = exchange(rows).reshape(groups, slabs, channels, 2, spectra, inputs)
    depth = 2 * slabs * spectra
    planes = turned.transpose(2, 3, 1, 4, 0, 5).reshape(channels, depth, groups * inputs)
    return correlate(
        functools.partial(plain_correlate_kernel, min(256, groups * inputs)),
        [pl.BlockSpec((1, depth, groups * inputs), lambda c: (c, 0, 0))],
        [planes],
        None,
        0,
        channels,
        out_shape,
        depth // 2,
    )


def shards(voltages, prototype):
    inputs, samples = voltages.shape
    taps, frame = prototype.shape
    spectra = samples // frame
    groups, slabs = lax.axis_size("inp"), lax.axis_size("tm")
    devices = groups * slabs
    channels = frame // 2 // devices
    total_inputs = groups * inputs
    out_shape = jax.ShapeDtypeStruct((channels, 2, total_inputs, total_inputs), jnp.bfloat16)
    earlier = shifted(voltages[:, (spectra - taps + 1) * frame :], "tm", 1)
    if inputs % LANES or channels % 16:
        return narrow(voltages, prototype, earlier, out_shape)

    middle = channels // 2
    last = 3 * channels // 16
    early = channels - middle - last
    blocks = spectra // ROWS
    unit = 2 * ROWS

    main = filter_main(voltages, prototype)
    rows = (blocks - 1) * early * unit
    table = table_of(frame, devices, channels, 0, early)
    first_turned = exchange(transform(table, main, devices, rows, 0, None))

    edge = filter_edge(voltages, earlier, prototype)
    rows = channels * unit + (blocks - 1) * middle * unit
    table = table_of(frame, devices, channels, 0, channels)
    buffer = transform(table, edge, devices, rows, 0, None)
    table = table_of(frame, devices, channels, early, middle)
    buffer = transform(table, main, devices, rows, channels * unit, buffer)
    middle_turned = exchange(buffer)

    rows = (blocks - 1) * last * unit
    table = table_of(frame, devices, channels, early + middle, last)
    last_turned = exchange(transform(table, main, devices, rows, 0, None))

    total = None
    first = 0
    for turned, count, base in (
        (first_turned, early, 0),
        (middle_turned, middle, channels),
        (last_turned, last, 0),
    ):
        shape = (devices, unit, inputs)
        in_specs = [pl.BlockSpec(shape, lambda c, first=first: (0, first + c, 0))]
        for b in range(blocks - 1):
            at = base + b * count
            in_specs.append(pl.BlockSpec(shape, lambda c, at=at: (0, at + c, 0)))
        operands = [middle_turned] + [turned] * (blocks - 1)
        kernel = functools.partial(correlate_kernel, min(256, total_inputs), slabs, blocks)
        total = correlate(
            kernel, in_specs, operands, total, first, count, out_shape, slabs * spectra
        )
        first += count
    return total


def solution(mesh):
    return jax.shard_map(
        shards,
        mesh=mesh,
        in_specs=(P("inp", "tm"), P()),
        out_specs=P(("inp", "tm"), None, None, None),
        check_vma=False,
    )
```

time: 478 us -> 439 us (0.918)
  waiting for transfers between devices: 301 us -> 279 us
  Pallas kernels: 143 us -> 128 us
    pallas_call x10 -> x9, Pallas kernels: 143 us -> 128 us  [the longest x3 53.8 us: correlate(): pl.pallas_call(kernel, grid=(count,), in_specs=in_specs, out_specs=pl.Blo...]
    ppermute x1, waiting for transfers between devices: 18.4 us -> 6.75 us  [shifted(): return lax.ppermute(block, axis, route)]
    all_to_all x4 -> x3, waiting for transfers between devices: 283 us -> 272 us  [exchange(): lax.all_to_all(rows, ('inp', 'tm'), split_axis=0, concat_axis=0, tiled=True)]
    all_to_all x4 -> x3, starting transfers between devices: 24.2 us -> 22.3 us  [exchange(): lax.all_to_all(rows, ('inp', 'tm'), split_axis=0, concat_axis=0, tiled=True)]
  transfers between devices with their start and end apart: 5 -> 4, of which waited for: 5 -> 4; matrix products, arithmetic and copies ran while one was open for 0% -> 0% of each run, Pallas kernels for 22% -> 27%
where the time goes in v2:
time: 439 us; the launch traced here: 438 us
  waiting for transfers between devices  279 us (64%)
  Pallas kernels  128 us (29%)
  starting transfers between devices  28.6 us (7%)
    all_to_all x3, waiting for transfers between devices, exchange(): lax.all_to_all(rows, ('inp', 'tm'), split_axis=0, concat_axis=0, tiled=True)  272 us
    pallas_call x3, Pallas kernels, correlate(): pl.pallas_call(kernel, grid=(count,), in_specs=in_specs, out_specs=pl.Blo...  53.8 us
    pallas_call x4, Pallas kernels, transform(): pl.pallas_call(functools.partial(dft_kernel, inputs), grid=(spectra // RO...  45.7 us
    all_to_all x3, starting transfers between devices, exchange(): lax.all_to_all(rows, ('inp', 'tm'), split_axis=0, concat_axis=0, tiled=True)  22.3 us
    pallas_call x1, Pallas kernels, filter_main(): pl.pallas_call(functools.partial(main_filter_kernel, taps, frame, spectra...  18.6 us
    pallas_call x1, Pallas kernels, filter_edge(): pl.pallas_call(functools.partial(edge_filter_kernel, taps, frame, ROWS),...  9.37 us
  transfers between devices with their start and end apart: 4, of which 4 were waited for; matrix products, arithmetic and copies ran while one was open for 0% of the time, Pallas kernels for 27%

profile of v2, /device:TPU:0, one launch (start us, length us, event | category | flops | bytes accessed | tf_op | source)
XLA Modules:
  0.0 437.9 jit_solution(13508703032180706736)
XLA Ops:
  0.0 2.9 slice.3
  2.9 6.2 %collective-permute-start = (bf16[128,7168]{1,0:T(8,128)(2,1)}, bf16[128,7168]{1,0:T(8,128)(2,1)}, u32[]{:S(2)}, u32[]{:S(2)}) collective-permute-start(bf16[128,7168]{1,0:T(8,128)(2,1)} %slice.3), channel_id=1, source_target_pairs={{0,1},{1,2},{2,3},{4,5},{5,6},{6,7},{8,9},{9,10},{10,11},{12,13},{... | collective-permute-start | bytes 5505032 | tf_op jit(solution)/shard_map/ppermute | solution.py:20
  9.1 18.6 %filter_main.1.f_ref = bf16[48,128,1024]{2,1,0:T(8,128)(2,1)} custom-call(bf16[128,65536]{1,0:T(8,128)(2,1)} %v_ref.3, f32[8,1024]{1,0:T(8,128)} %p_ref.3), custom_call_target="tpu_custom_call" | custom-call | flops 134217728 | bytes 33554432 | tf_op jit(solution)/shard_map/filter_main/pallas_call | solution.py:87
  27.7 10.4 %dft.7 = bf16[32,480,128]{2,1,0:T(8,128)(2,1)} custom-call(bf16[320,1024]{1,0:T(8,128)(2,1)} %constant.8.clone.t_ref, bf16[48,128,1024]{2,1,0:T(8,128)(2,1)} %filter_main.1.f_ref), custom_call_target="tpu_custom_call" | custom-call | flops 16106127360 | bytes 16515072 | tf_op jit(solution)/shard_map/dft/pallas_call | solution.py:161
  38.1 3.7 all-to-all-start.2
  41.7 6.8 %collective-permute-done.e_ref = bf16[128,7168]{1,0:T(8,128)(2,1)} collective-permute-done((bf16[128,7168]{1,0:T(8,128)(2,1)}, bf16[128,7168]{1,0:T(8,128)(2,1)}, u32[]{:S(2)}, u32[]{:S(2)}) %collective-permute-start) | collective-permute-done | bytes 1835040 | tf_op jit(solution)/shard_map/ppermute | solution.py:20
  48.5 9.4 %filter_edge.1.f_ref = bf16[16,128,1024]{2,1,0:T(8,128)(2,1)} custom-call(bf16[128,65536]{1,0:T(8,128)(2,1)} %v_ref.3, bf16[128,7168]{1,0:T(8,128)(2,1)} %collective-permute-done.e_ref, f32[8,1024]{1,0:T(8,128)} %p_ref.3), custom_call_target="tpu_custom_call" | custom-call | flops 68719476736 | bytes 12582912 | tf_op jit(solution)/shard_map/filter_edge/pallas_call | solution.py:109
  57.9 10.0 %dft.4.refs_0_ = bf16[32,1280,128]{2,1,0:T(8,128)(2,1)} custom-call(bf16[1024,1024]{1,0:T(8,128)(2,1)} %constant.9.clone.t_ref, bf16[16,128,1024]{2,1,0:T(8,128)(2,1)} %filter_edge.1.f_ref), custom_call_target="tpu_custom_call" | custom-call | flops 17179869184 | bytes 8388608 | tf_op jit(solution)/shard_map/dft/pallas_call | solution.py:161
  67.9 16.1 %dft.5 = bf16[32,1280,128]{2,1,0:T(8,128)(2,1)} custom-call(bf16[512,1024]{1,0:T(8,128)(2,1)} %constant.10.clone.t_ref, bf16[48,128,1024]{2,1,0:T(8,128)(2,1)} %filter_main.1.f_ref, bf16[32,1280,128]{2,1,0:T(8,128)(2,1)} %dft.4.refs_0_), custom_call_target="tpu_custom_call", output_to_operand_aliasing={{}: (2, {})} | custom-call | flops 25769803776 | bytes 18874368 | tf_op jit(solution)/shard_map/dft/pallas_call | solution.py:161
  84.0 44.5 %all-to-all-done.2.refs_1_.refs_2_.refs_3_ = bf16[32,480,128]{2,1,0:T(8,128)(2,1)} async-done(((bf16[32,480,128]{2,1,0:T(8,128)(2,1)}), bf16[32,480,128]{2,1,0:T(8,128)(2,1)}, u32[]{:S(2)}, u32[]{:S(2)}) %all-to-all-start.2) | async-done | bytes 3932192 | tf_op jit(solution)/shard_map/all_to_all | solution.py:255
  128.5 8.6 %all-to-all-start = ((bf16[32,1280,128]{2,1,0:T(8,128)(2,1)}), bf16[32,1280,128]{2,1,0:T(8,128)(2,1)}, u32[]{:S(2)}, u32[]{:S(2)}) async-start(bf16[32,1280,128]{2,1,0:T(8,128)(2,1)} %dft.5), calls=%async_computation | async-start | bytes 20971520 | tf_op jit(solution)/shard_map/all_to_all | solution.py:255
  137.1 9.2 %dft.6 = bf16[32,288,128]{2,1,0:T(8,128)(2,1)} custom-call(bf16[192,1024]{1,0:T(8,128)(2,1)} %constant.11.clone.t_ref, bf16[48,128,1024]{2,1,0:T(8,128)(2,1)} %filter_main.1.f_ref), custom_call_target="tpu_custom_call" | custom-call | flops 9663676416 | bytes 14942208 | tf_op jit(solution)/shard_map/dft/pallas_call | solution.py:161
  146.3 217.0 %all-to-all-done.refs_0_.refs_1_.refs_2_.refs_3_ = bf16[32,1280,128]{2,1,0:T(8,128)(2,1)} async-done(((bf16[32,1280,128]{2,1,0:T(8,128)(2,1)}), bf16[32,1280,128]{2,1,0:T(8,128)(2,1)}, u32[]{:S(2)}, u32[]{:S(2)}) %all-to-all-start) | async-done | bytes 10485792 | tf_op jit(solution)/shard_map/all_to_all | solution.py:255
  363.2 10.1 %all-to-all-start.1 = ((bf16[32,288,128]{2,1,0:T(8,128)(2,1)}), bf16[32,288,128]{2,1,0:T(8,128)(2,1)}, u32[]{:S(2)}, u32[]{:S(2)}) async-start(bf16[32,288,128]{2,1,0:T(8,128)(2,1)} %dft.6), calls=%async_computation.1 | async-start | bytes 4718592 | tf_op jit(solution)/shard_map/all_to_all | solution.py:255
  373.3 17.0 %correlate.3.refs_4_ = bf16[16,2,1024,1024]{3,2,1,0:T(8,128)(2,1)} custom-call(bf16[32,1280,128]{2,1,0:T(8,128)(2,1)} %all-to-all-done.refs_0_.refs_1_.refs_2_.refs_3_, bf16[32,480,128]{2,1,0:T(8,128)(2,1)} %all-to-all-done.2.refs_1_.refs_2_.refs_3_, bf16[32,480,128]{2,1,0:T(8,128)(2,1)} %all-to-all-done.2.refs_1_.refs_2_.refs_3_, ...), custom_call_target="tpu_custom_call" | custom-call | flops 10737418240 | bytes 26214400 | tf_op jit(solution)/shard_map/correlate/pallas_call | solution.py:227
  390.3 25.4 %correlate.4.refs_4_ = bf16[16,2,1024,1024]{3,2,1,0:T(8,128)(2,1)} custom-call(bf16[32,1280,128]{2,1,0:T(8,128)(2,1)} %all-to-all-done.refs_0_.refs_1_.refs_2_.refs_3_, bf16[32,1280,128]{2,1,0:T(8,128)(2,1)} %all-to-all-done.refs_0_.refs_1_.refs_2_.refs_3_, ...), custom_call_target="tpu_custom_call", output_to_operand_aliasing={{}: (4, {})} | custom-call | flops 17179869184 | bytes 41943040 | tf_op jit(solution)/shard_map/correlate/pallas_call | solution.py:227
  415.7 10.7 %all-to-all-done.1.refs_1_.refs_2_.refs_3_ = bf16[32,288,128]{2,1,0:T(8,128)(2,1)} async-done(((bf16[32,288,128]{2,1,0:T(8,128)(2,1)}), bf16[32,288,128]{2,1,0:T(8,128)(2,1)}, u32[]{:S(2)}, u32[]{:S(2)}) %all-to-all-start.1) | async-done | bytes 2359328 | tf_op jit(solution)/shard_map/all_to_all | solution.py:255
  426.4 11.5 %correlate.5 = bf16[16,2,1024,1024]{3,2,1,0:T(8,128)(2,1)} custom-call(bf16[32,1280,128]{2,1,0:T(8,128)(2,1)} %all-to-all-done.refs_0_.refs_1_.refs_2_.refs_3_, bf16[32,288,128]{2,1,0:T(8,128)(2,1)} %all-to-all-done.1.refs_1_.refs_2_.refs_3_, bf16[32,288,128]{2,1,0:T(8,128)(2,1)} %all-to-all-done.1.refs_1_.refs_2_.refs_3_, ...), custom_call_target="tpu_custom_call", output_to_operand_aliasing={{}: (4, {})} | custom-call | flops 6442450944 | bytes 15728640 | tf_op jit(solution)/shard_map/correlate/pallas_call | solution.py:227
Async XLA Ops:
  2.9 45.6 %collective-permute-start = (bf16[128,7168]{1,0:T(8,128)(2,1)}, bf16[128,7168]{1,0:T(8,128)(2,1)}, u32[]{:S(2)}, u32[]{:S(2)}) collective-permute-start(bf16[128,7168]{1,0:T(8,128)(2,1)} %slice.3), channel_id=1, source_target_pairs={{0,1},{1,2},{2,3},{4,5},{5,6},{6,7},{8,9},{9,10},{10,11},{12,13},{... | collective-permute-start | bytes 5505032 | tf_op jit(solution)/shard_map/ppermute | solution.py:20
  38.1 90.4 %all-to-all-start.2 = ((bf16[32,480,128]{2,1,0:T(8,128)(2,1)}), bf16[32,480,128]{2,1,0:T(8,128)(2,1)}, u32[]{:S(2)}, u32[]{:S(2)}) async-start(bf16[32,480,128]{2,1,0:T(8,128)(2,1)} %dft.7), calls=%async_computation.2 | async-start | bytes 7864320 | tf_op jit(solution)/shard_map/all_to_all | solution.py:255
  128.5 234.8 %all-to-all-start = ((bf16[32,1280,128]{2,1,0:T(8,128)(2,1)}), bf16[32,1280,128]{2,1,0:T(8,128)(2,1)}, u32[]{:S(2)}, u32[]{:S(2)}) async-start(bf16[32,1280,128]{2,1,0:T(8,128)(2,1)} %dft.5), calls=%async_computation | async-start | bytes 20971520 | tf_op jit(solution)/shard_map/all_to_all | solution.py:255
  363.2 63.2 %all-to-all-start.1 = ((bf16[32,288,128]{2,1,0:T(8,128)(2,1)}), bf16[32,288,128]{2,1,0:T(8,128)(2,1)}, u32[]{:S(2)}, u32[]{:S(2)}) async-start(bf16[32,288,128]{2,1,0:T(8,128)(2,1)} %dft.6), calls=%async_computation.1 | async-start | bytes 4718592 | tf_op jit(solution)/shard_map/all_to_all | solution.py:255

commit v3 on v2

--- a/solution.py
+++ b/solution.py
@@ -11,6 +11,7 @@
 LANES = 128
 ROWS = 16
 VMEM = 63 * 1024 * 1024
+VMEM_FIRST = 56 * 1024 * 1024
 WEIGHT = 8
 
 
@@ -93,7 +94,7 @@
         ],
         out_specs=pl.BlockSpec((spectra - ROWS, ROWS, frame), lambda r: (0, r, 0)),
         out_shape=jax.ShapeDtypeStruct((spectra - ROWS, inputs, frame), jnp.bfloat16),
-        compiler_params=pltpu.CompilerParams(vmem_limit_bytes=VMEM),
+        compiler_params=pltpu.CompilerParams(vmem_limit_bytes=VMEM_FIRST),
         cost_estimate=pl.CostEstimate(
             flops=2 * taps * inputs * samples,
             bytes_accessed=4 * inputs * samples,
@@ -142,13 +143,13 @@
     o_ref[...] = turn[...].reshape(o_ref.shape).astype(jnp.bfloat16)
 
 
-def transform(table, filtered, devices, rows, first, buffer):
+def transform(table, filtered, devices, rows, first, buffer, vmem=VMEM):
     spectra, inputs, frame = filtered.shape
     columns = table.shape[0]
     height = columns // devices * ROWS
     assert first % height == 0
     split = 1
-    while columns // split > 320 and devices % (2 * split) == 0:
+    while columns // split > 384 and devices % (2 * split) == 0:
         split *= 2
     in_specs = [
         pl.BlockSpec((columns // split, frame), lambda b, d: (d, 0)),
@@ -168,7 +169,7 @@
         out_shape=jax.ShapeDtypeStruct((devices, rows, inputs), jnp.bfloat16),
         input_output_aliases={} if buffer is None else {2: 0},
         scratch_shapes=[pltpu.VMEM((columns // split * ROWS, inputs), jnp.float32)],
-        compiler_params=pltpu.CompilerParams(vmem_limit_bytes=VMEM),
+        compiler_params=pltpu.CompilerParams(vmem_limit_bytes=vmem),
         cost_estimate=pl.CostEstimate(
             flops=WEIGHT * columns * spectra * inputs * frame,
             bytes_accessed=2 * spectra * inputs * (frame + columns),
@@ -178,43 +179,72 @@
     )(*operands)
 
 
-def correlate_block(block, o_ref, right, left):
-    depth, inputs = right.shape
+def pipelined(block, count, fill, o_ref, slots):
+    step = pl.program_id(0)
+    depth, inputs = slots[0][0].shape
     spectra = depth // 2
-    power = jnp.zeros((ROWS, inputs), jnp.float32)
-    for at in range(0, depth, ROWS):
-        piece = right[pl.ds(at, ROWS), :].astype(jnp.float32)
-        power = power + piece * piece
-    across = lax.rsqrt(jnp.sum(power, axis=0, keepdims=True) + 1e-06)
-    down = jnp.broadcast_to(across, (8, inputs)).T[:, :1]
-    left[...] = right[...].T
-    for at in range(0, inputs, block):
+
+    def prepare(at, slot):
+        right, left, across = slot
+        columns = pl.ds(at, block)
+        fill(at, right)
+        power = jnp.zeros((ROWS, block), jnp.float32)
+        for row in range(0, depth, ROWS):
+            piece = right[pl.ds(row, ROWS), columns].astype(jnp.float32)
+            power = power + piece * piece
+        scale = lax.rsqrt(jnp.sum(power, axis=0, keepdims=True) + 1e-06)
+        across[:, columns] = jnp.broadcast_to(scale, (8, block))
+        left[columns, :] = right[:, columns].T
+
+    def multiply(at, slot):
+        right, left, across = slot
         rows = pl.ds(at, block)
         own = left[rows, :]
         swapped = jnp.concatenate([own[:, spectra:], -own[:, :spectra]], axis=1)
+        down = across[:, rows].T[:, :1]
         for part, operand in enumerate((own, swapped)):
             gram = jnp.dot(operand, right[...], preferred_element_type=jnp.float32)
-            o_ref[0, part, rows, :] = (gram * down[at : at + block] * across).astype(jnp.bfloat16)
-
-
-def correlate_kernel(block, slabs, count, *refs):
-    blocks, o_ref, right, left = refs[:count], refs[-3], refs[-2], refs[-1]
-    devices, _, width = blocks[0].shape
-    spectra = right.shape[0] // 2
-    for part in range(2):
-        for device in range(devices):
-            g, t = device // slabs, device % slabs
-            for b, ref in enumerate(blocks):
-                at = part * spectra + (t * len(blocks) + b) * ROWS
-                right[pl.ds(at, ROWS), pl.ds(g * width, width)] = ref[
-                    device, pl.ds(part * ROWS, ROWS), :
-                ]
-    correlate_block(block, o_ref, right, left)
-
-
-def plain_correlate_kernel(block, r_ref, o_ref, right, left):
-    right[...] = r_ref[0]
-    correlate_block(block, o_ref, right, left)
+            o_ref[0, part, rows, :] = (gram * down * across[:1, :]).astype(jnp.bfloat16)
+
+    def both(old, new):
+        for at in range(0, inputs, block):
+            if old is not None:
+                multiply(at, old)
+            if new is not None:
+                prepare(at, new)
+
+    even, odd = slots
+    inside = (step > 0) & (step < count)
+    pl.when(step == 0)(lambda: both(None, even))
+    pl.when(inside & (step % 2 == 1))(lambda: both(even, odd))
+    pl.when(inside & (step % 2 == 0))(lambda: both(odd, even))
+    pl.when(step == count)(lambda: both(slots[(count - 1) % 2], None))
+
+
+def correlate_kernel(block, count, slabs, blocks, *refs):
+    sources, o_ref, slots = refs[:blocks], refs[-7], (refs[-6:-3], refs[-3:])
+    devices, _, width = sources[0].shape
+    spectra = slots[0][0].shape[0] // 2
+
+    def fill(first, right):
+        for part in range(2):
+            for device in range(first // width * slabs, (first + block) // width * slabs):
+                g, t = device // slabs, device % slabs
+                for b, ref in enumerate(sources):
+                    at = part * spectra + (t * blocks + b) * ROWS
+                    right[pl.ds(at, ROWS), pl.ds(g * width, width)] = ref[
+                        device, pl.ds(part * ROWS, ROWS), :
+                    ]
+
+    pipelined(block, count, fill, o_ref, slots)
+
+
+def plain_correlate_kernel(block, count, r_ref, o_ref, *scratch):
+    def fill(first, right):
+        columns = pl.ds(first, block)
+        right[:, columns] = r_ref[0, :, columns]
+
+    pipelined(block, count, fill, o_ref, (scratch[:3], scratch[3:]))
 
 
 def correlate(kernel, in_specs, operands, total, first, count, out_shape, spectra):
@@ -224,17 +254,21 @@
         aliases = {len(operands): 0}
         in_specs = [*in_specs, pl.BlockSpec(memory_space=pl.ANY)]
         operands = [*operands, total]
+    slot = [
+        pltpu.VMEM((2 * spectra, inputs), jnp.bfloat16),
+        pltpu.VMEM((inputs, 2 * spectra), jnp.bfloat16),
+        pltpu.VMEM((8, inputs), jnp.float32),
+    ]
     return pl.pallas_call(
         kernel,
-        grid=(count,),
+        grid=(count + 1,),
         in_specs=in_specs,
-        out_specs=pl.BlockSpec((1, 2, inputs, inputs), lambda c: (first + c, 0, 0, 0)),
+        out_specs=pl.BlockSpec(
+            (1, 2, inputs, inputs), lambda c: (first + jnp.maximum(c - 1, 0), 0, 0, 0)
+        ),
         out_shape=out_shape,
         input_output_aliases=aliases,
-        scratch_shapes=[
-            pltpu.VMEM((2 * spectra, inputs), jnp.bfloat16),
-            pltpu.VMEM((inputs, 2 * spectra), jnp.bfloat16),
-        ],
+        scratch_shapes=slot + slot,
         compiler_params=pltpu.CompilerParams(vmem_limit_bytes=VMEM),
         cost_estimate=pl.CostEstimate(
             flops=8 * count * inputs * inputs * spectra,
@@ -272,8 +306,12 @@
     depth = 2 * slabs * spectra
     planes = turned.transpose(2, 3, 1, 4, 0, 5).reshape(channels, depth, groups * inputs)
     return correlate(
-        functools.partial(plain_correlate_kernel, min(256, groups * inputs)),
-        [pl.BlockSpec((1, depth, groups * inputs), lambda c: (c, 0, 0))],
+        functools.partial(plain_correlate_kernel, min(256, groups * inputs), channels),
+        [
+            pl.BlockSpec(
+                (1, depth, groups * inputs), lambda c: (jnp.minimum(c, channels - 1), 0, 0)
+            )
+        ],
         [planes],
         None,
         0,
@@ -297,7 +335,7 @@
         return narrow(voltages, prototype, earlier, out_shape)
 
     middle = channels // 2
-    last = 3 * channels // 16
+    last = channels // 8
     early = channels - middle - last
     blocks = spectra // ROWS
     unit = 2 * ROWS
@@ -305,7 +343,7 @@
     main = filter_main(voltages, prototype)
     rows = (blocks - 1) * early * unit
     table = table_of(frame, devices, channels, 0, early)
-    first_turned = exchange(transform(table, main, devices, rows, 0, None))
+    first_turned = exchange(transform(table, main, devices, rows, 0, None, VMEM_FIRST))
 
     edge = filter_edge(voltages, earlier, prototype)
     rows = channels * unit + (blocks - 1) * middle * unit
@@ -326,13 +364,18 @@
         (middle_turned, middle, channels),
         (last_turned, last, 0),
     ):
-        shape = (devices, unit, inputs)
-        in_specs = [pl.BlockSpec(shape, lambda c, first=first: (0, first + c, 0))]
-        for b in range(blocks - 1):
-            at = base + b * count
-            in_specs.append(pl.BlockSpec(shape, lambda c, at=at: (0, at + c, 0)))
+        bases = [first] + [base + b * count for b in range(blocks - 1)]
+        in_specs = [
+            pl.BlockSpec(
+                (devices, unit, inputs),
+                lambda c, at=at, end=count - 1: (0, at + jnp.minimum(c, end), 0),
+            )
+            for at in bases
+        ]
         operands = [middle_turned] + [turned] * (blocks - 1)
-        kernel = functools.partial(correlate_kernel, min(256, total_inputs), slabs, blocks)
+        kernel = functools.partial(
+            correlate_kernel, min(256, total_inputs), count, slabs, blocks
+        )
         total = correlate(
             kernel, in_specs, operands, total, first, count, out_shape, slabs * spectra
         )

time: 439 us -> 443 us (level)
  waiting for transfers between devices: 279 us -> 285 us
    all_to_all x3, waiting for transfers between devices: 272 us -> 280 us  [exchange(): lax.all_to_all(rows, ('inp', 'tm'), split_axis=0, concat_axis=0, tiled=True)]
  transfers between devices with their start and end apart: 4 -> 4, of which waited for: 4 -> 3; matrix products, arithmetic and copies ran while one was open for 0% -> 0% of each run, Pallas kernels for 27% -> 27%
where the time goes in v3:
time: 443 us; the launch traced here: 442 us
  waiting for transfers between devices  285 us (64%)
  Pallas kernels  128 us (29%)
  starting transfers between devices  27.8 us (6%)
    all_to_all x3, waiting for transfers between devices, exchange(): lax.all_to_all(rows, ('inp', 'tm'), split_axis=0, concat_axis=0, tiled=True)  280 us
    pallas_call x3, Pallas kernels, correlate(): pl.pallas_call(kernel, grid=(count + 1,), in_specs=in_specs, out_specs=pl...  53.5 us
    pallas_call x4, Pallas kernels, transform(): pl.pallas_call(functools.partial(dft_kernel, inputs), grid=(spectra // RO...  46.2 us
    all_to_all x3, starting transfers between devices, exchange(): lax.all_to_all(rows, ('inp', 'tm'), split_axis=0, concat_axis=0, tiled=True)  21.6 us
    pallas_call x1, Pallas kernels, filter_main(): pl.pallas_call(functools.partial(main_filter_kernel, taps, frame, spectra...  18.6 us
    pallas_call x1, Pallas kernels, filter_edge(): pl.pallas_call(functools.partial(edge_filter_kernel, taps, frame, ROWS),...  9.38 us
  transfers between devices with their start and end apart: 4, of which 3 were waited for; matrix products, arithmetic and copies ran while one was open for 0% of the time, Pallas kernels for 27%

profile of v3, /device:TPU:0, one launch (start us, length us, event | category | flops | bytes accessed | tf_op | source)
XLA Modules:
  0.0 442.4 jit_solution(12086349647646457690)
XLA Ops:
  0.0 1.6 slice.3
  1.6 6.2 %collective-permute-start = (bf16[128,7168]{1,0:T(8,128)(2,1)S(1)}, bf16[128,7168]{1,0:T(8,128)(2,1)}, u32[]{:S(2)}, u32[]{:S(2)}) collective-permute-start(bf16[128,7168]{1,0:T(8,128)(2,1)S(1)} %slice.3), channel_id=1, source_target_pairs={{0,1},{1,2},{2,3},{4,5},{5,6},{6,7},{8,9},{9,10},{10,11},{12,13},{... | collective-permute-start | bytes 5505032 | tf_op jit(solution)/shard_map/ppermute | solution.py:21
  7.8 18.6 %filter_main.1.f_ref = bf16[48,128,1024]{2,1,0:T(8,128)(2,1)} custom-call(bf16[128,65536]{1,0:T(8,128)(2,1)} %v_ref.3, f32[8,1024]{1,0:T(8,128)} %p_ref.3), custom_call_target="tpu_custom_call" | custom-call | flops 134217728 | bytes 33554432 | tf_op jit(solution)/shard_map/filter_main/pallas_call | solution.py:88
  26.4 11.4 %dft.7 = bf16[32,576,128]{2,1,0:T(8,128)(2,1)} custom-call(bf16[384,1024]{1,0:T(8,128)(2,1)} %constant.8.clone.t_ref, bf16[48,128,1024]{2,1,0:T(8,128)(2,1)} %filter_main.1.f_ref), custom_call_target="tpu_custom_call" | custom-call | flops 19327352832 | bytes 17301504 | tf_op jit(solution)/shard_map/dft/pallas_call | solution.py:162
  37.8 3.7 all-to-all-start.2
  41.5 5.5 %collective-permute-done.e_ref = bf16[128,7168]{1,0:T(8,128)(2,1)} collective-permute-done((bf16[128,7168]{1,0:T(8,128)(2,1)S(1)}, bf16[128,7168]{1,0:T(8,128)(2,1)}, u32[]{:S(2)}, u32[]{:S(2)}) %collective-permute-start) | collective-permute-done | bytes 1835040 | tf_op jit(solution)/shard_map/ppermute | solution.py:21
  47.0 9.4 %filter_edge.1.f_ref = bf16[16,128,1024]{2,1,0:T(8,128)(2,1)} custom-call(bf16[128,65536]{1,0:T(8,128)(2,1)} %v_ref.3, bf16[128,7168]{1,0:T(8,128)(2,1)} %collective-permute-done.e_ref, f32[8,1024]{1,0:T(8,128)} %p_ref.3), custom_call_target="tpu_custom_call" | custom-call | flops 68719476736 | bytes 12582912 | tf_op jit(solution)/shard_map/filter_edge/pallas_call | solution.py:110
  56.3 10.0 %dft.4.refs_0_ = bf16[32,1280,128]{2,1,0:T(8,128)(2,1)} custom-call(bf16[1024,1024]{1,0:T(8,128)(2,1)} %constant.9.clone.t_ref, bf16[16,128,1024]{2,1,0:T(8,128)(2,1)} %filter_edge.1.f_ref), custom_call_target="tpu_custom_call" | custom-call | flops 17179869184 | bytes 8388608 | tf_op jit(solution)/shard_map/dft/pallas_call | solution.py:162
  66.4 16.1 %dft.5 = bf16[32,1280,128]{2,1,0:T(8,128)(2,1)} custom-call(bf16[512,1024]{1,0:T(8,128)(2,1)} %constant.10.clone.t_ref, bf16[48,128,1024]{2,1,0:T(8,128)(2,1)} %filter_main.1.f_ref, bf16[32,1280,128]{2,1,0:T(8,128)(2,1)} %dft.4.refs_0_), custom_call_target="tpu_custom_call", output_to_operand_aliasing={{}: (2, {})} | custom-call | flops 25769803776 | bytes 18874368 | tf_op jit(solution)/shard_map/dft/pallas_call | solution.py:162
  82.4 62.4 %all-to-all-done.2.refs_1_.refs_2_.refs_3_ = bf16[32,576,128]{2,1,0:T(8,128)(2,1)} async-done(((bf16[32,576,128]{2,1,0:T(8,128)(2,1)}), bf16[32,576,128]{2,1,0:T(8,128)(2,1)}, u32[]{:S(2)}, u32[]{:S(2)}) %all-to-all-start.2) | async-done | bytes 4718624 | tf_op jit(solution)/shard_map/all_to_all | solution.py:289
  144.9 7.8 %all-to-all-start = ((bf16[32,1280,128]{2,1,0:T(8,128)(2,1)}), bf16[32,1280,128]{2,1,0:T(8,128)(2,1)}, u32[]{:S(2)}, u32[]{:S(2)}) async-start(bf16[32,1280,128]{2,1,0:T(8,128)(2,1)} %dft.5), calls=%async_computation | async-start | bytes 20971520 | tf_op jit(solution)/shard_map/all_to_all | solution.py:289
  152.7 8.7 %dft.6 = bf16[32,192,128]{2,1,0:T(8,128)(2,1)} custom-call(bf16[128,1024]{1,0:T(8,128)(2,1)} %constant.11.clone.t_ref, bf16[48,128,1024]{2,1,0:T(8,128)(2,1)} %filter_main.1.f_ref), custom_call_target="tpu_custom_call" | custom-call | flops 6442450944 | bytes 14155776 | tf_op jit(solution)/shard_map/dft/pallas_call | solution.py:162
  161.4 217.4 %all-to-all-done.refs_0_.refs_1_.refs_2_.refs_3_ = bf16[32,1280,128]{2,1,0:T(8,128)(2,1)} async-done(((bf16[32,1280,128]{2,1,0:T(8,128)(2,1)}), bf16[32,1280,128]{2,1,0:T(8,128)(2,1)}, u32[]{:S(2)}, u32[]{:S(2)}) %all-to-all-start) | async-done | bytes 10485792 | tf_op jit(solution)/shard_map/all_to_all | solution.py:289
  378.9 10.1 %all-to-all-start.1 = ((bf16[32,192,128]{2,1,0:T(8,128)(2,1)}), bf16[32,192,128]{2,1,0:T(8,128)(2,1)}, u32[]{:S(2)}, u32[]{:S(2)}) async-start(bf16[32,192,128]{2,1,0:T(8,128)(2,1)} %dft.6), calls=%async_computation.1 | async-start | bytes 3145728 | tf_op jit(solution)/shard_map/all_to_all | solution.py:289
  388.9 19.4 %correlate.3.refs_4_ = bf16[16,2,1024,1024]{3,2,1,0:T(8,128)(2,1)} custom-call(bf16[32,1280,128]{2,1,0:T(8,128)(2,1)} %all-to-all-done.refs_0_.refs_1_.refs_2_.refs_3_, bf16[32,576,128]{2,1,0:T(8,128)(2,1)} %all-to-all-done.2.refs_1_.refs_2_.refs_3_, bf16[32,576,128]{2,1,0:T(8,128)(2,1)} %all-to-all-done.2.refs_1_.refs_2_.refs_3_, ...), custom_call_target="tpu_custom_call" | custom-call | flops 12884901888 | bytes 31457280 | tf_op jit(solution)/shard_map/correlate/pallas_call | solution.py:262
  408.3 25.0 %correlate.4.refs_4_ = bf16[16,2,1024,1024]{3,2,1,0:T(8,128)(2,1)} custom-call(bf16[32,1280,128]{2,1,0:T(8,128)(2,1)} %all-to-all-done.refs_0_.refs_1_.refs_2_.refs_3_, bf16[32,1280,128]{2,1,0:T(8,128)(2,1)} %all-to-all-done.refs_0_.refs_1_.refs_2_.refs_3_, ...), custom_call_target="tpu_custom_call", output_to_operand_aliasing={{}: (4, {})} | custom-call | flops 17179869184 | bytes 41943040 | tf_op jit(solution)/shard_map/correlate/pallas_call | solution.py:262
  433.3 0.0 all-to-all-done.1.refs_1_.refs_2_.refs_3_
  433.3 9.1 %correlate.5 = bf16[16,2,1024,1024]{3,2,1,0:T(8,128)(2,1)} custom-call(bf16[32,1280,128]{2,1,0:T(8,128)(2,1)} %all-to-all-done.refs_0_.refs_1_.refs_2_.refs_3_, bf16[32,192,128]{2,1,0:T(8,128)(2,1)} %all-to-all-done.1.refs_1_.refs_2_.refs_3_, bf16[32,192,128]{2,1,0:T(8,128)(2,1)} %all-to-all-done.1.refs_1_.refs_2_.refs_3_, ...), custom_call_target="tpu_custom_call", output_to_operand_aliasing={{}: (4, {})} | custom-call | flops 4294967296 | bytes 10485760 | tf_op jit(solution)/shard_map/correlate/pallas_call | solution.py:262
Async XLA Ops:
  1.6 45.3 %collective-permute-start = (bf16[128,7168]{1,0:T(8,128)(2,1)S(1)}, bf16[128,7168]{1,0:T(8,128)(2,1)}, u32[]{:S(2)}, u32[]{:S(2)}) collective-permute-start(bf16[128,7168]{1,0:T(8,128)(2,1)S(1)} %slice.3), channel_id=1, source_target_pairs={{0,1},{1,2},{2,3},{4,5},{5,6},{6,7},{8,9},{9,10},{10,11},{12,13},{... | collective-permute-start | bytes 5505032 | tf_op jit(solution)/shard_map/ppermute | solution.py:21
  37.8 107.1 %all-to-all-start.2 = ((bf16[32,576,128]{2,1,0:T(8,128)(2,1)}), bf16[32,576,128]{2,1,0:T(8,128)(2,1)}, u32[]{:S(2)}, u32[]{:S(2)}) async-start(bf16[32,576,128]{2,1,0:T(8,128)(2,1)} %dft.7), calls=%async_computation.2 | async-start | bytes 9437184 | tf_op jit(solution)/shard_map/all_to_all | solution.py:289
  144.9 234.0 %all-to-all-start = ((bf16[32,1280,128]{2,1,0:T(8,128)(2,1)}), bf16[32,1280,128]{2,1,0:T(8,128)(2,1)}, u32[]{:S(2)}, u32[]{:S(2)}) async-start(bf16[32,1280,128]{2,1,0:T(8,128)(2,1)} %dft.5), calls=%async_computation | async-start | bytes 20971520 | tf_op jit(solution)/shard_map/all_to_all | solution.py:289
  378.9 54.5 %all-to-all-start.1 = ((bf16[32,192,128]{2,1,0:T(8,128)(2,1)}), bf16[32,192,128]{2,1,0:T(8,128)(2,1)}, u32[]{:S(2)}, u32[]{:S(2)}) async-start(bf16[32,192,128]{2,1,0:T(8,128)(2,1)} %dft.6), calls=%async_computation.1 | async-start | bytes 3145728 | tf_op jit(solution)/shard_map/all_to_all | solution.py:289

commit v4 on v3

--- a/solution.py
+++ b/solution.py
@@ -198,13 +198,17 @@
 
     def multiply(at, slot):
         right, left, across = slot
-        rows = pl.ds(at, block)
+        rows, columns = pl.ds(at, block), pl.ds(at, inputs - at)
         own = left[rows, :]
         swapped = jnp.concatenate([own[:, spectra:], -own[:, :spectra]], axis=1)
         down = across[:, rows].T[:, :1]
         for part, operand in enumerate((own, swapped)):
-            gram = jnp.dot(operand, right[...], preferred_element_type=jnp.float32)
-            o_ref[0, part, rows, :] = (gram * down * across[:1, :]).astype(jnp.bfloat16)
+            gram = jnp.dot(operand, right[:, columns], preferred_element_type=jnp.float32)
+            scaled = (gram * down * across[:1, columns]).astype(jnp.bfloat16)
+            o_ref[0, part, rows, columns] = scaled
+            for below in range(at + block, inputs, block):
+                mirror = scaled[:, below - at : below - at + block].T
+                o_ref[0, part, pl.ds(below, block), rows] = -mirror if part else mirror
 
     def both(old, new):
         for at in range(0, inputs, block):

time: 443 us -> 434 us (0.980)
  Pallas kernels: 128 us -> 115 us
    pallas_call x3, Pallas kernels: 53.5 us -> 40.8 us  [correlate(): pl.pallas_call(kernel, grid=(count + 1,), in_specs=in_specs, out_specs=pl...]
  transfers between devices with their start and end apart: 4 -> 4, of which waited for: 3 -> 4; matrix products, arithmetic and copies ran while one was open for 0% -> 0% of each run, Pallas kernels for 27% -> 25%
where the time goes in v4:
time: 434 us; the launch traced here: 432 us
  waiting for transfers between devices  288 us (66%)
  Pallas kernels  115 us (26%)
  starting transfers between devices  27.8 us (6%)
    all_to_all x3, waiting for transfers between devices, exchange(): lax.all_to_all(rows, ('inp', 'tm'), split_axis=0, concat_axis=0, tiled=True)  282 us
    pallas_call x4, Pallas kernels, transform(): pl.pallas_call(functools.partial(dft_kernel, inputs), grid=(spectra // RO...  46.2 us
    pallas_call x3, Pallas kernels, correlate(): pl.pallas_call(kernel, grid=(count + 1,), in_specs=in_specs, out_specs=pl...  40.8 us
    all_to_all x3, starting transfers between devices, exchange(): lax.all_to_all(rows, ('inp', 'tm'), split_axis=0, concat_axis=0, tiled=True)  21.6 us
    pallas_call x1, Pallas kernels, filter_main(): pl.pallas_call(functools.partial(main_filter_kernel, taps, frame, spectra...  18.6 us
    pallas_call x1, Pallas kernels, filter_edge(): pl.pallas_call(functools.partial(edge_filter_kernel, taps, frame, ROWS),...  9.38 us
  transfers between devices with their start and end apart: 4, of which 4 were waited for; matrix products, arithmetic and copies ran while one was open for 0% of the time, Pallas kernels for 25%

profile of v4, /device:TPU:0, one launch (start us, length us, event | category | flops | bytes accessed | tf_op | source)
XLA Modules:
  0.0 431.9 jit_solution(8124509794393240872)
XLA Ops:
  0.0 1.6 slice.3
  1.6 6.2 %collective-permute-start = (bf16[128,7168]{1,0:T(8,128)(2,1)S(1)}, bf16[128,7168]{1,0:T(8,128)(2,1)}, u32[]{:S(2)}, u32[]{:S(2)}) collective-permute-start(bf16[128,7168]{1,0:T(8,128)(2,1)S(1)} %slice.3), channel_id=1, source_target_pairs={{0,1},{1,2},{2,3},{4,5},{5,6},{6,7},{8,9},{9,10},{10,11},{12,13},{... | collective-permute-start | bytes 5505032 | tf_op jit(solution)/shard_map/ppermute | solution.py:21
  7.8 18.6 %filter_main.1.f_ref = bf16[48,128,1024]{2,1,0:T(8,128)(2,1)} custom-call(bf16[128,65536]{1,0:T(8,128)(2,1)} %v_ref.3, f32[8,1024]{1,0:T(8,128)} %p_ref.3), custom_call_target="tpu_custom_call" | custom-call | flops 134217728 | bytes 33554432 | tf_op jit(solution)/shard_map/filter_main/pallas_call | solution.py:88
  26.4 11.4 %dft.7 = bf16[32,576,128]{2,1,0:T(8,128)(2,1)} custom-call(bf16[384,1024]{1,0:T(8,128)(2,1)} %constant.8.clone.t_ref, bf16[48,128,1024]{2,1,0:T(8,128)(2,1)} %filter_main.1.f_ref), custom_call_target="tpu_custom_call" | custom-call | flops 19327352832 | bytes 17301504 | tf_op jit(solution)/shard_map/dft/pallas_call | solution.py:162
  37.8 3.7 all-to-all-start.2
  41.5 5.5 %collective-permute-done.e_ref = bf16[128,7168]{1,0:T(8,128)(2,1)} collective-permute-done((bf16[128,7168]{1,0:T(8,128)(2,1)S(1)}, bf16[128,7168]{1,0:T(8,128)(2,1)}, u32[]{:S(2)}, u32[]{:S(2)}) %collective-permute-start) | collective-permute-done | bytes 1835040 | tf_op jit(solution)/shard_map/ppermute | solution.py:21
  47.0 9.4 %filter_edge.1.f_ref = bf16[16,128,1024]{2,1,0:T(8,128)(2,1)} custom-call(bf16[128,65536]{1,0:T(8,128)(2,1)} %v_ref.3, bf16[128,7168]{1,0:T(8,128)(2,1)} %collective-permute-done.e_ref, f32[8,1024]{1,0:T(8,128)} %p_ref.3), custom_call_target="tpu_custom_call" | custom-call | flops 68719476736 | bytes 12582912 | tf_op jit(solution)/shard_map/filter_edge/pallas_call | solution.py:110
  56.3 10.0 %dft.4.refs_0_ = bf16[32,1280,128]{2,1,0:T(8,128)(2,1)} custom-call(bf16[1024,1024]{1,0:T(8,128)(2,1)} %constant.9.clone.t_ref, bf16[16,128,1024]{2,1,0:T(8,128)(2,1)} %filter_edge.1.f_ref), custom_call_target="tpu_custom_call" | custom-call | flops 17179869184 | bytes 8388608 | tf_op jit(solution)/shard_map/dft/pallas_call | solution.py:162
  66.4 16.1 %dft.5 = bf16[32,1280,128]{2,1,0:T(8,128)(2,1)} custom-call(bf16[512,1024]{1,0:T(8,128)(2,1)} %constant.10.clone.t_ref, bf16[48,128,1024]{2,1,0:T(8,128)(2,1)} %filter_main.1.f_ref, bf16[32,1280,128]{2,1,0:T(8,128)(2,1)} %dft.4.refs_0_), custom_call_target="tpu_custom_call", output_to_operand_aliasing={{}: (2, {})} | custom-call | flops 25769803776 | bytes 18874368 | tf_op jit(solution)/shard_map/dft/pallas_call | solution.py:162
  82.4 62.4 %all-to-all-done.2.refs_1_.refs_2_.refs_3_ = bf16[32,576,128]{2,1,0:T(8,128)(2,1)} async-done(((bf16[32,576,128]{2,1,0:T(8,128)(2,1)}), bf16[32,576,128]{2,1,0:T(8,128)(2,1)}, u32[]{:S(2)}, u32[]{:S(2)}) %all-to-all-start.2) | async-done | bytes 4718624 | tf_op jit(solution)/shard_map/all_to_all | solution.py:293
  144.9 7.8 %all-to-all-start = ((bf16[32,1280,128]{2,1,0:T(8,128)(2,1)}), bf16[32,1280,128]{2,1,0:T(8,128)(2,1)}, u32[]{:S(2)}, u32[]{:S(2)}) async-start(bf16[32,1280,128]{2,1,0:T(8,128)(2,1)} %dft.5), calls=%async_computation | async-start | bytes 20971520 | tf_op jit(solution)/shard_map/all_to_all | solution.py:293
  152.7 8.7 %dft.6 = bf16[32,192,128]{2,1,0:T(8,128)(2,1)} custom-call(bf16[128,1024]{1,0:T(8,128)(2,1)} %constant.11.clone.t_ref, bf16[48,128,1024]{2,1,0:T(8,128)(2,1)} %filter_main.1.f_ref), custom_call_target="tpu_custom_call" | custom-call | flops 6442450944 | bytes 14155776 | tf_op jit(solution)/shard_map/dft/pallas_call | solution.py:162
  161.4 217.4 %all-to-all-done.refs_0_.refs_1_.refs_2_.refs_3_ = bf16[32,1280,128]{2,1,0:T(8,128)(2,1)} async-done(((bf16[32,1280,128]{2,1,0:T(8,128)(2,1)}), bf16[32,1280,128]{2,1,0:T(8,128)(2,1)}, u32[]{:S(2)}, u32[]{:S(2)}) %all-to-all-start) | async-done | bytes 10485792 | tf_op jit(solution)/shard_map/all_to_all | solution.py:293
  378.9 10.1 %all-to-all-start.1 = ((bf16[32,192,128]{2,1,0:T(8,128)(2,1)}), bf16[32,192,128]{2,1,0:T(8,128)(2,1)}, u32[]{:S(2)}, u32[]{:S(2)}) async-start(bf16[32,192,128]{2,1,0:T(8,128)(2,1)} %dft.6), calls=%async_computation.1 | async-start | bytes 3145728 | tf_op jit(solution)/shard_map/all_to_all | solution.py:293
  388.9 14.9 %correlate.3.refs_4_ = bf16[16,2,1024,1024]{3,2,1,0:T(8,128)(2,1)} custom-call(bf16[32,1280,128]{2,1,0:T(8,128)(2,1)} %all-to-all-done.refs_0_.refs_1_.refs_2_.refs_3_, bf16[32,576,128]{2,1,0:T(8,128)(2,1)} %all-to-all-done.2.refs_1_.refs_2_.refs_3_, bf16[32,576,128]{2,1,0:T(8,128)(2,1)} %all-to-all-done.2.refs_1_.refs_2_.refs_3_, ...), custom_call_target="tpu_custom_call" | custom-call | flops 12884901888 | bytes 31457280 | tf_op jit(solution)/shard_map/correlate/pallas_call | solution.py:266
  403.8 18.7 %correlate.4.refs_4_ = bf16[16,2,1024,1024]{3,2,1,0:T(8,128)(2,1)} custom-call(bf16[32,1280,128]{2,1,0:T(8,128)(2,1)} %all-to-all-done.refs_0_.refs_1_.refs_2_.refs_3_, bf16[32,1280,128]{2,1,0:T(8,128)(2,1)} %all-to-all-done.refs_0_.refs_1_.refs_2_.refs_3_, ...), custom_call_target="tpu_custom_call", output_to_operand_aliasing={{}: (4, {})} | custom-call | flops 17179869184 | bytes 41943040 | tf_op jit(solution)/shard_map/correlate/pallas_call | solution.py:266
  422.5 2.2 all-to-all-done.1.refs_1_.refs_2_.refs_3_
  424.7 7.2 %correlate.5 = bf16[16,2,1024,1024]{3,2,1,0:T(8,128)(2,1)} custom-call(bf16[32,1280,128]{2,1,0:T(8,128)(2,1)} %all-to-all-done.refs_0_.refs_1_.refs_2_.refs_3_, bf16[32,192,128]{2,1,0:T(8,128)(2,1)} %all-to-all-done.1.refs_1_.refs_2_.refs_3_, bf16[32,192,128]{2,1,0:T(8,128)(2,1)} %all-to-all-done.1.refs_1_.refs_2_.refs_3_, ...), custom_call_target="tpu_custom_call", output_to_operand_aliasing={{}: (4, {})} | custom-call | flops 4294967296 | bytes 10485760 | tf_op jit(solution)/shard_map/correlate/pallas_call | solution.py:266
Async XLA Ops:
  1.6 45.3 %collective-permute-start = (bf16[128,7168]{1,0:T(8,128)(2,1)S(1)}, bf16[128,7168]{1,0:T(8,128)(2,1)}, u32[]{:S(2)}, u32[]{:S(2)}) collective-permute-start(bf16[128,7168]{1,0:T(8,128)(2,1)S(1)} %slice.3), channel_id=1, source_target_pairs={{0,1},{1,2},{2,3},{4,5},{5,6},{6,7},{8,9},{9,10},{10,11},{12,13},{... | collective-permute-start | bytes 5505032 | tf_op jit(solution)/shard_map/ppermute | solution.py:21
  37.8 107.1 %all-to-all-start.2 = ((bf16[32,576,128]{2,1,0:T(8,128)(2,1)}), bf16[32,576,128]{2,1,0:T(8,128)(2,1)}, u32[]{:S(2)}, u32[]{:S(2)}) async-start(bf16[32,576,128]{2,1,0:T(8,128)(2,1)} %dft.7), calls=%async_computation.2 | async-start | bytes 9437184 | tf_op jit(solution)/shard_map/all_to_all | solution.py:293
  144.9 234.0 %all-to-all-start = ((bf16[32,1280,128]{2,1,0:T(8,128)(2,1)}), bf16[32,1280,128]{2,1,0:T(8,128)(2,1)}, u32[]{:S(2)}, u32[]{:S(2)}) async-start(bf16[32,1280,128]{2,1,0:T(8,128)(2,1)} %dft.5), calls=%async_computation | async-start | bytes 20971520 | tf_op jit(solution)/shard_map/all_to_all | solution.py:293
  378.9 45.8 %all-to-all-start.1 = ((bf16[32,192,128]{2,1,0:T(8,128)(2,1)}), bf16[32,192,128]{2,1,0:T(8,128)(2,1)}, u32[]{:S(2)}, u32[]{:S(2)}) async-start(bf16[32,192,128]{2,1,0:T(8,128)(2,1)} %dft.6), calls=%async_computation.1 | async-start | bytes 3145728 | tf_op jit(solution)/shard_map/all_to_all | solution.py:293

commit v5 on v3

--- a/solution.py
+++ b/solution.py
@@ -194,17 +194,25 @@
             power = power + piece * piece
         scale = lax.rsqrt(jnp.sum(power, axis=0, keepdims=True) + 1e-06)
         across[:, columns] = jnp.broadcast_to(scale, (8, block))
-        left[columns, :] = right[:, columns].T
+        turned = right[:, columns].T
+        left[pl.ds(2 * at, block), :] = turned
+        left[pl.ds(2 * at + block, block), pl.ds(0, spectra)] = turned[:, spectra:]
+        left[pl.ds(2 * at + block, block), pl.ds(spectra, spectra)] = -turned[:, :spectra]
 
     def multiply(at, slot):
         right, left, across = slot
         rows = pl.ds(at, block)
-        own = left[rows, :]
-        swapped = jnp.concatenate([own[:, spectra:], -own[:, :spectra]], axis=1)
+        operand = left[pl.ds(2 * at, 2 * block), :]
         down = across[:, rows].T[:, :1]
-        for part, operand in enumerate((own, swapped)):
-            gram = jnp.dot(operand, right[...], preferred_element_type=jnp.float32)
-            o_ref[0, part, rows, :] = (gram * down * across[:1, :]).astype(jnp.bfloat16)
+        for other in range(at, inputs, block):
+            columns = pl.ds(other, block)
+            gram = jnp.dot(operand, right[:, columns], preferred_element_type=jnp.float32)
+            for part in range(2):
+                own = gram[part * block : (part + 1) * block]
+                scaled = (own * down * across[:1, columns]).astype(jnp.bfloat16)
+                o_ref[0, part, rows, columns] = scaled
+                if other > at:
+                    o_ref[0, part, columns, rows] = -scaled.T if part else scaled.T
 
     def both(old, new):
         for at in range(0, inputs, block):
@@ -256,7 +264,7 @@
         operands = [*operands, total]
     slot = [
         pltpu.VMEM((2 * spectra, inputs), jnp.bfloat16),
-        pltpu.VMEM((inputs, 2 * spectra), jnp.bfloat16),
+        pltpu.VMEM((2 * inputs, 2 * spectra), jnp.bfloat16),
         pltpu.VMEM((8, inputs), jnp.float32),
     ]
     return pl.pallas_call(

time: 443 us -> 435 us (0.982)
  Pallas kernels: 128 us -> 116 us
    pallas_call x3, Pallas kernels: 53.5 us -> 41.7 us  [correlate(): pl.pallas_call(kernel, grid=(count + 1,), in_specs=in_specs, out_specs=pl...]
  transfers between devices with their start and end apart: 4 -> 4, of which waited for: 3 -> 4; matrix products, arithmetic and copies ran while one was open for 0% -> 0% of each run, Pallas kernels for 27% -> 25%
where the time goes in v5:
time: 435 us; the launch traced here: 432 us
  waiting for transfers between devices  287 us (66%)
  Pallas kernels  116 us (27%)
  starting transfers between devices  27.8 us (6%)
    all_to_all x3, waiting for transfers between devices, exchange(): lax.all_to_all(rows, ('inp', 'tm'), split_axis=0, concat_axis=0, tiled=True)  281 us
    pallas_call x4, Pallas kernels, transform(): pl.pallas_call(functools.partial(dft_kernel, inputs), grid=(spectra // RO...  46.2 us
    pallas_call x3, Pallas kernels, correlate(): pl.pallas_call(kernel, grid=(count + 1,), in_specs=in_specs, out_specs=pl...  41.7 us
    all_to_all x3, starting transfers between devices, exchange(): lax.all_to_all(rows, ('inp', 'tm'), split_axis=0, concat_axis=0, tiled=True)  21.6 us
    pallas_call x1, Pallas kernels, filter_main(): pl.pallas_call(functools.partial(main_filter_kernel, taps, frame, spectra...  18.6 us
    pallas_call x1, Pallas kernels, filter_edge(): pl.pallas_call(functools.partial(edge_filter_kernel, taps, frame, ROWS),...  9.38 us
  transfers between devices with their start and end apart: 4, of which 4 were waited for; matrix products, arithmetic and copies ran while one was open for 0% of the time, Pallas kernels for 25%

profile of v5, /device:TPU:0, one launch (start us, length us, event | category | flops | bytes accessed | tf_op | source)
XLA Modules:
  0.0 432.1 jit_solution(6890551265832423045)
XLA Ops:
  0.0 1.6 slice.3
  1.6 6.2 %collective-permute-start = (bf16[128,7168]{1,0:T(8,128)(2,1)S(1)}, bf16[128,7168]{1,0:T(8,128)(2,1)}, u32[]{:S(2)}, u32[]{:S(2)}) collective-permute-start(bf16[128,7168]{1,0:T(8,128)(2,1)S(1)} %slice.3), channel_id=1, source_target_pairs={{0,1},{1,2},{2,3},{4,5},{5,6},{6,7},{8,9},{9,10},{10,11},{12,13},{... | collective-permute-start | bytes 5505032 | tf_op jit(solution)/shard_map/ppermute | solution.py:21
  7.8 18.6 %filter_main.1.f_ref = bf16[48,128,1024]{2,1,0:T(8,128)(2,1)} custom-call(bf16[128,65536]{1,0:T(8,128)(2,1)} %v_ref.3, f32[8,1024]{1,0:T(8,128)} %p_ref.3), custom_call_target="tpu_custom_call" | custom-call | flops 134217728 | bytes 33554432 | tf_op jit(solution)/shard_map/filter_main/pallas_call | solution.py:88
  26.4 11.4 %dft.7 = bf16[32,576,128]{2,1,0:T(8,128)(2,1)} custom-call(bf16[384,1024]{1,0:T(8,128)(2,1)} %constant.8.clone.t_ref, bf16[48,128,1024]{2,1,0:T(8,128)(2,1)} %filter_main.1.f_ref), custom_call_target="tpu_custom_call" | custom-call | flops 19327352832 | bytes 17301504 | tf_op jit(solution)/shard_map/dft/pallas_call | solution.py:162
  37.8 3.7 all-to-all-start.2
  41.5 5.5 %collective-permute-done.e_ref = bf16[128,7168]{1,0:T(8,128)(2,1)} collective-permute-done((bf16[128,7168]{1,0:T(8,128)(2,1)S(1)}, bf16[128,7168]{1,0:T(8,128)(2,1)}, u32[]{:S(2)}, u32[]{:S(2)}) %collective-permute-start) | collective-permute-done | bytes 1835040 | tf_op jit(solution)/shard_map/ppermute | solution.py:21
  47.0 9.4 %filter_edge.1.f_ref = bf16[16,128,1024]{2,1,0:T(8,128)(2,1)} custom-call(bf16[128,65536]{1,0:T(8,128)(2,1)} %v_ref.3, bf16[128,7168]{1,0:T(8,128)(2,1)} %collective-permute-done.e_ref, f32[8,1024]{1,0:T(8,128)} %p_ref.3), custom_call_target="tpu_custom_call" | custom-call | flops 68719476736 | bytes 12582912 | tf_op jit(solution)/shard_map/filter_edge/pallas_call | solution.py:110
  56.3 10.0 %dft.4.refs_0_ = bf16[32,1280,128]{2,1,0:T(8,128)(2,1)} custom-call(bf16[1024,1024]{1,0:T(8,128)(2,1)} %constant.9.clone.t_ref, bf16[16,128,1024]{2,1,0:T(8,128)(2,1)} %filter_edge.1.f_ref), custom_call_target="tpu_custom_call" | custom-call | flops 17179869184 | bytes 8388608 | tf_op jit(solution)/shard_map/dft/pallas_call | solution.py:162
  66.4 16.1 %dft.5 = bf16[32,1280,128]{2,1,0:T(8,128)(2,1)} custom-call(bf16[512,1024]{1,0:T(8,128)(2,1)} %constant.10.clone.t_ref, bf16[48,128,1024]{2,1,0:T(8,128)(2,1)} %filter_main.1.f_ref, bf16[32,1280,128]{2,1,0:T(8,128)(2,1)} %dft.4.refs_0_), custom_call_target="tpu_custom_call", output_to_operand_aliasing={{}: (2, {})} | custom-call | flops 25769803776 | bytes 18874368 | tf_op jit(solution)/shard_map/dft/pallas_call | solution.py:162
  82.4 62.4 %all-to-all-done.2.refs_1_.refs_2_.refs_3_ = bf16[32,576,128]{2,1,0:T(8,128)(2,1)} async-done(((bf16[32,576,128]{2,1,0:T(8,128)(2,1)}), bf16[32,576,128]{2,1,0:T(8,128)(2,1)}, u32[]{:S(2)}, u32[]{:S(2)}) %all-to-all-start.2) | async-done | bytes 4718624 | tf_op jit(solution)/shard_map/all_to_all | solution.py:297
  144.9 7.8 %all-to-all-start = ((bf16[32,1280,128]{2,1,0:T(8,128)(2,1)}), bf16[32,1280,128]{2,1,0:T(8,128)(2,1)}, u32[]{:S(2)}, u32[]{:S(2)}) async-start(bf16[32,1280,128]{2,1,0:T(8,128)(2,1)} %dft.5), calls=%async_computation | async-start | bytes 20971520 | tf_op jit(solution)/shard_map/all_to_all | solution.py:297
  152.7 8.7 %dft.6 = bf16[32,192,128]{2,1,0:T(8,128)(2,1)} custom-call(bf16[128,1024]{1,0:T(8,128)(2,1)} %constant.11.clone.t_ref, bf16[48,128,1024]{2,1,0:T(8,128)(2,1)} %filter_main.1.f_ref), custom_call_target="tpu_custom_call" | custom-call | flops 6442450944 | bytes 14155776 | tf_op jit(solution)/shard_map/dft/pallas_call | solution.py:162
  161.4 217.4 %all-to-all-done.refs_0_.refs_1_.refs_2_.refs_3_ = bf16[32,1280,128]{2,1,0:T(8,128)(2,1)} async-done(((bf16[32,1280,128]{2,1,0:T(8,128)(2,1)}), bf16[32,1280,128]{2,1,0:T(8,128)(2,1)}, u32[]{:S(2)}, u32[]{:S(2)}) %all-to-all-start) | async-done | bytes 10485792 | tf_op jit(solution)/shard_map/all_to_all | solution.py:297
  378.9 10.1 %all-to-all-start.1 = ((bf16[32,192,128]{2,1,0:T(8,128)(2,1)}), bf16[32,192,128]{2,1,0:T(8,128)(2,1)}, u32[]{:S(2)}, u32[]{:S(2)}) async-start(bf16[32,192,128]{2,1,0:T(8,128)(2,1)} %dft.6), calls=%async_computation.1 | async-start | bytes 3145728 | tf_op jit(solution)/shard_map/all_to_all | solution.py:297
  388.9 15.2 %correlate.3.refs_4_ = bf16[16,2,1024,1024]{3,2,1,0:T(8,128)(2,1)} custom-call(bf16[32,1280,128]{2,1,0:T(8,128)(2,1)} %all-to-all-done.refs_0_.refs_1_.refs_2_.refs_3_, bf16[32,576,128]{2,1,0:T(8,128)(2,1)} %all-to-all-done.2.refs_1_.refs_2_.refs_3_, bf16[32,576,128]{2,1,0:T(8,128)(2,1)} %all-to-all-done.2.refs_1_.refs_2_.refs_3_, ...), custom_call_target="tpu_custom_call" | custom-call | flops 12884901888 | bytes 31457280 | tf_op jit(solution)/shard_map/correlate/pallas_call | solution.py:270
  404.1 19.2 %correlate.4.refs_4_ = bf16[16,2,1024,1024]{3,2,1,0:T(8,128)(2,1)} custom-call(bf16[32,1280,128]{2,1,0:T(8,128)(2,1)} %all-to-all-done.refs_0_.refs_1_.refs_2_.refs_3_, bf16[32,1280,128]{2,1,0:T(8,128)(2,1)} %all-to-all-done.refs_0_.refs_1_.refs_2_.refs_3_, ...), custom_call_target="tpu_custom_call", output_to_operand_aliasing={{}: (4, {})} | custom-call | flops 17179869184 | bytes 41943040 | tf_op jit(solution)/shard_map/correlate/pallas_call | solution.py:270
  423.3 1.4 all-to-all-done.1.refs_1_.refs_2_.refs_3_
  424.7 7.4 %correlate.5 = bf16[16,2,1024,1024]{3,2,1,0:T(8,128)(2,1)} custom-call(bf16[32,1280,128]{2,1,0:T(8,128)(2,1)} %all-to-all-done.refs_0_.refs_1_.refs_2_.refs_3_, bf16[32,192,128]{2,1,0:T(8,128)(2,1)} %all-to-all-done.1.refs_1_.refs_2_.refs_3_, bf16[32,192,128]{2,1,0:T(8,128)(2,1)} %all-to-all-done.1.refs_1_.refs_2_.refs_3_, ...), custom_call_target="tpu_custom_call", output_to_operand_aliasing={{}: (4, {})} | custom-call | flops 4294967296 | bytes 10485760 | tf_op jit(solution)/shard_map/correlate/pallas_call | solution.py:270
Async XLA Ops:
  1.6 45.3 %collective-permute-start = (bf16[128,7168]{1,0:T(8,128)(2,1)S(1)}, bf16[128,7168]{1,0:T(8,128)(2,1)}, u32[]{:S(2)}, u32[]{:S(2)}) collective-permute-start(bf16[128,7168]{1,0:T(8,128)(2,1)S(1)} %slice.3), channel_id=1, source_target_pairs={{0,1},{1,2},{2,3},{4,5},{5,6},{6,7},{8,9},{9,10},{10,11},{12,13},{... | collective-permute-start | bytes 5505032 | tf_op jit(solution)/shard_map/ppermute | solution.py:21
  37.8 107.1 %all-to-all-start.2 = ((bf16[32,576,128]{2,1,0:T(8,128)(2,1)}), bf16[32,576,128]{2,1,0:T(8,128)(2,1)}, u32[]{:S(2)}, u32[]{:S(2)}) async-start(bf16[32,576,128]{2,1,0:T(8,128)(2,1)} %dft.7), calls=%async_computation.2 | async-start | bytes 9437184 | tf_op jit(solution)/shard_map/all_to_all | solution.py:297
  144.9 234.0 %all-to-all-start = ((bf16[32,1280,128]{2,1,0:T(8,128)(2,1)}), bf16[32,1280,128]{2,1,0:T(8,128)(2,1)}, u32[]{:S(2)}, u32[]{:S(2)}) async-start(bf16[32,1280,128]{2,1,0:T(8,128)(2,1)} %dft.5), calls=%async_computation | async-start | bytes 20971520 | tf_op jit(solution)/shard_map/all_to_all | solution.py:297
  378.9 45.8 %all-to-all-start.1 = ((bf16[32,192,128]{2,1,0:T(8,128)(2,1)}), bf16[32,192,128]{2,1,0:T(8,128)(2,1)}, u32[]{:S(2)}, u32[]{:S(2)}) async-start(bf16[32,192,128]{2,1,0:T(8,128)(2,1)} %dft.6), calls=%async_computation.1 | async-start | bytes 3145728 | tf_op jit(solution)/shard_map/all_to_all | solution.py:297

commit v6 on v4

--- a/solution.py
+++ b/solution.py
@@ -228,17 +228,18 @@
 def correlate_kernel(block, count, slabs, blocks, *refs):
     sources, o_ref, slots = refs[:blocks], refs[-7], (refs[-6:-3], refs[-3:])
     devices, _, width = sources[0].shape
+    groups = devices // slabs
     spectra = slots[0][0].shape[0] // 2
 
     def fill(first, right):
         for part in range(2):
-            for device in range(first // width * slabs, (first + block) // width * slabs):
-                g, t = device // slabs, device % slabs
-                for b, ref in enumerate(sources):
-                    at = part * spectra + (t * blocks + b) * ROWS
-                    right[pl.ds(at, ROWS), pl.ds(g * width, width)] = ref[
-                        device, pl.ds(part * ROWS, ROWS), :
-                    ]
+            for g in range(first // width, (first + block) // width):
+                for t in range(slabs):
+                    for b, ref in enumerate(sources):
+                        at = part * spectra + (t * blocks + b) * ROWS
+                        right[pl.ds(at, ROWS), pl.ds(g * width, width)] = ref[
+                            t * groups + g, pl.ds(part * ROWS, ROWS), :
+                        ]
 
     pipelined(block, count, fill, o_ref, slots)
 
@@ -283,14 +284,15 @@
     )(*operands)
 
 
-def table_of(frame, devices, channels, first, count):
-    channel = np.arange(devices)[:, None, None] * channels + first
+def table_of(frame, groups, slabs, channels, first, count):
+    device = np.arange(groups)[None, :] * slabs + np.arange(slabs)[:, None]
+    channel = device.reshape(-1, 1, 1) * channels + first
     channel = channel + np.arange(count)[None, :, None]
     return dft_rows(frame, (2 * channel + np.arange(2)[None, None, :]).reshape(-1))
 
 
 def exchange(rows):
-    return lax.all_to_all(rows, ("inp", "tm"), split_axis=0, concat_axis=0, tiled=True)
+    return lax.all_to_all(rows, ("tm", "inp"), split_axis=0, concat_axis=0, tiled=True)
 
 
 def narrow(voltages, prototype, earlier, out_shape):
@@ -302,13 +304,13 @@
     filtered = jnp.concatenate(
         [filter_edge(voltages, earlier, prototype), filter_main(voltages, prototype)]
     )
-    table = table_of(frame, devices, channels, 0, channels)
+    table = table_of(frame, groups, slabs, channels, 0, channels)
     dims = (((1,), (2,)), ((), ()))
     rows = lax.dot_general(table, filtered, dims, preferred_element_type=jnp.float32)
     rows = rows.astype(jnp.bfloat16).reshape(devices, -1, inputs)
-    turned = exchange(rows).reshape(groups, slabs, channels, 2, spectra, inputs)
+    turned = exchange(rows).reshape(slabs, groups, channels, 2, spectra, inputs)
     depth = 2 * slabs * spectra
-    planes = turned.transpose(2, 3, 1, 4, 0, 5).reshape(channels, depth, groups * inputs)
+    planes = turned.transpose(2, 3, 0, 4, 1, 5).reshape(channels, depth, groups * inputs)
     return correlate(
         functools.partial(plain_correlate_kernel, min(256, groups * inputs), channels),
         [
@@ -346,19 +348,19 @@
 
     main = filter_main(voltages, prototype)
     rows = (blocks - 1) * early * unit
-    table = table_of(frame, devices, channels, 0, early)
+    table = table_of(frame, groups, slabs, channels, 0, early)
     first_turned = exchange(transform(table, main, devices, rows, 0, None, VMEM_FIRST))
 
     edge = filter_edge(voltages, earlier, prototype)
     rows = channels * unit + (blocks - 1) * middle * unit
-    table = table_of(frame, devices, channels, 0, channels)
+    table = table_of(frame, groups, slabs, channels, 0, channels)
     buffer = transform(table, edge, devices, rows, 0, None)
-    table = table_of(frame, devices, channels, early, middle)
+    table = table_of(frame, groups, slabs, channels, early, middle)
     buffer = transform(table, main, devices, rows, channels * unit, buffer)
     middle_turned = exchange(buffer)
 
     rows = (blocks - 1) * last * unit
-    table = table_of(frame, devices, channels, early + middle, last)
+    table = table_of(frame, groups, slabs, channels, early + middle, last)
     last_turned = exchange(transform(table, main, devices, rows, 0, None))
 
     total = None

time: 434 us -> 437 us (level)
  waiting for transfers between devices: 288 us -> 298 us
  starting transfers between devices: 27.8 us -> 20.7 us
    all_to_all x3, waiting for transfers between devices: 282 us -> 293 us  [exchange(): lax.all_to_all(rows, ('tm', 'inp'), split_axis=0, concat_axis=0, tiled=True)]
    all_to_all x3, starting transfers between devices: 21.6 us -> 14.5 us  [exchange(): lax.all_to_all(rows, ('tm', 'inp'), split_axis=0, concat_axis=0, tiled=True)]
where the time goes in v6:
time: 437 us; the launch traced here: 435 us
  waiting for transfers between devices  298 us (68%)
  Pallas kernels  115 us (26%)
  starting transfers between devices  20.7 us (5%)
    all_to_all x3, waiting for transfers between devices, exchange(): lax.all_to_all(rows, ('tm', 'inp'), split_axis=0, concat_axis=0, tiled=True)  293 us
    pallas_call x4, Pallas kernels, transform(): pl.pallas_call(functools.partial(dft_kernel, inputs), grid=(spectra // RO...  46.2 us
    pallas_call x3, Pallas kernels, correlate(): pl.pallas_call(kernel, grid=(count + 1,), in_specs=in_specs, out_specs=pl...  40.8 us
    pallas_call x1, Pallas kernels, filter_main(): pl.pallas_call(functools.partial(main_filter_kernel, taps, frame, spectra...  18.6 us
    all_to_all x3, starting transfers between devices, exchange(): lax.all_to_all(rows, ('tm', 'inp'), split_axis=0, concat_axis=0, tiled=True)  14.5 us
    pallas_call x1, Pallas kernels, filter_edge(): pl.pallas_call(functools.partial(edge_filter_kernel, taps, frame, ROWS),...  9.38 us
  transfers between devices with their start and end apart: 4, of which 4 were waited for; matrix products, arithmetic and copies ran while one was open for 0% of the time, Pallas kernels for 25%

profile of v6, /device:TPU:0, one launch (start us, length us, event | category | flops | bytes accessed | tf_op | source)
XLA Modules:
  0.0 435.5 jit_solution(9897416243292587502)
XLA Ops:
  0.0 1.6 slice.3
  1.6 6.2 %collective-permute-start = (bf16[128,7168]{1,0:T(8,128)(2,1)S(1)}, bf16[128,7168]{1,0:T(8,128)(2,1)}, u32[]{:S(2)}, u32[]{:S(2)}) collective-permute-start(bf16[128,7168]{1,0:T(8,128)(2,1)S(1)} %slice.3), channel_id=1, source_target_pairs={{0,1},{1,2},{2,3},{4,5},{5,6},{6,7},{8,9},{9,10},{10,11},{12,13},{... | collective-permute-start | bytes 5505032 | tf_op jit(solution)/shard_map/ppermute | solution.py:21
  7.8 18.6 %filter_main.1.f_ref = bf16[48,128,1024]{2,1,0:T(8,128)(2,1)} custom-call(bf16[128,65536]{1,0:T(8,128)(2,1)} %v_ref.3, f32[8,1024]{1,0:T(8,128)} %p_ref.3), custom_call_target="tpu_custom_call" | custom-call | flops 134217728 | bytes 33554432 | tf_op jit(solution)/shard_map/filter_main/pallas_call | solution.py:88
  26.4 11.4 %dft.7 = bf16[32,576,128]{2,1,0:T(8,128)(2,1)} custom-call(bf16[384,1024]{1,0:T(8,128)(2,1)} %constant.8.clone.t_ref, bf16[48,128,1024]{2,1,0:T(8,128)(2,1)} %filter_main.1.f_ref), custom_call_target="tpu_custom_call" | custom-call | flops 19327352832 | bytes 17301504 | tf_op jit(solution)/shard_map/dft/pallas_call | solution.py:162
  37.8 3.7 all-to-all-start.2
  41.5 5.5 %collective-permute-done.e_ref = bf16[128,7168]{1,0:T(8,128)(2,1)} collective-permute-done((bf16[128,7168]{1,0:T(8,128)(2,1)S(1)}, bf16[128,7168]{1,0:T(8,128)(2,1)}, u32[]{:S(2)}, u32[]{:S(2)}) %collective-permute-start) | collective-permute-done | bytes 1835040 | tf_op jit(solution)/shard_map/ppermute | solution.py:21
  47.0 9.4 %filter_edge.1.f_ref = bf16[16,128,1024]{2,1,0:T(8,128)(2,1)} custom-call(bf16[128,65536]{1,0:T(8,128)(2,1)} %v_ref.3, bf16[128,7168]{1,0:T(8,128)(2,1)} %collective-permute-done.e_ref, f32[8,1024]{1,0:T(8,128)} %p_ref.3), custom_call_target="tpu_custom_call" | custom-call | flops 68719476736 | bytes 12582912 | tf_op jit(solution)/shard_map/filter_edge/pallas_call | solution.py:110
  56.3 10.0 %dft.4.refs_0_ = bf16[32,1280,128]{2,1,0:T(8,128)(2,1)} custom-call(bf16[1024,1024]{1,0:T(8,128)(2,1)} %constant.9.clone.t_ref, bf16[16,128,1024]{2,1,0:T(8,128)(2,1)} %filter_edge.1.f_ref), custom_call_target="tpu_custom_call" | custom-call | flops 17179869184 | bytes 8388608 | tf_op jit(solution)/shard_map/dft/pallas_call | solution.py:162
  66.4 16.1 %dft.5 = bf16[32,1280,128]{2,1,0:T(8,128)(2,1)} custom-call(bf16[512,1024]{1,0:T(8,128)(2,1)} %constant.10.clone.t_ref, bf16[48,128,1024]{2,1,0:T(8,128)(2,1)} %filter_main.1.f_ref, bf16[32,1280,128]{2,1,0:T(8,128)(2,1)} %dft.4.refs_0_), custom_call_target="tpu_custom_call", output_to_operand_aliasing={{}: (2, {})} | custom-call | flops 25769803776 | bytes 18874368 | tf_op jit(solution)/shard_map/dft/pallas_call | solution.py:162
  82.4 65.0 %all-to-all-done.2.refs_1_.refs_2_.refs_3_ = bf16[32,576,128]{2,1,0:T(8,128)(2,1)} async-done(((bf16[32,576,128]{2,1,0:T(8,128)(2,1)}), bf16[32,576,128]{2,1,0:T(8,128)(2,1)}, u32[]{:S(2)}, u32[]{:S(2)}) %all-to-all-start.2) | async-done | bytes 4718624 | tf_op jit(solution)/shard_map/all_to_all | solution.py:295
  147.4 7.2 %all-to-all-start = ((bf16[32,1280,128]{2,1,0:T(8,128)(2,1)}), bf16[32,1280,128]{2,1,0:T(8,128)(2,1)}, u32[]{:S(2)}, u32[]{:S(2)}) async-start(bf16[32,1280,128]{2,1,0:T(8,128)(2,1)} %dft.5), calls=%async_computation | async-start | bytes 20971520 | tf_op jit(solution)/shard_map/all_to_all | solution.py:295
  154.6 8.7 %dft.6 = bf16[32,192,128]{2,1,0:T(8,128)(2,1)} custom-call(bf16[128,1024]{1,0:T(8,128)(2,1)} %constant.11.clone.t_ref, bf16[48,128,1024]{2,1,0:T(8,128)(2,1)} %filter_main.1.f_ref), custom_call_target="tpu_custom_call" | custom-call | flops 6442450944 | bytes 14155776 | tf_op jit(solution)/shard_map/dft/pallas_call | solution.py:162
  163.4 223.5 %all-to-all-done.refs_0_.refs_1_.refs_2_.refs_3_ = bf16[32,1280,128]{2,1,0:T(8,128)(2,1)} async-done(((bf16[32,1280,128]{2,1,0:T(8,128)(2,1)}), bf16[32,1280,128]{2,1,0:T(8,128)(2,1)}, u32[]{:S(2)}, u32[]{:S(2)}) %all-to-all-start) | async-done | bytes 10485792 | tf_op jit(solution)/shard_map/all_to_all | solution.py:295
  386.9 3.6 all-to-all-start.1
  390.5 14.9 %correlate.3.refs_4_ = bf16[16,2,1024,1024]{3,2,1,0:T(8,128)(2,1)} custom-call(bf16[32,1280,128]{2,1,0:T(8,128)(2,1)} %all-to-all-done.refs_0_.refs_1_.refs_2_.refs_3_, bf16[32,576,128]{2,1,0:T(8,128)(2,1)} %all-to-all-done.2.refs_1_.refs_2_.refs_3_, bf16[32,576,128]{2,1,0:T(8,128)(2,1)} %all-to-all-done.2.refs_1_.refs_2_.refs_3_, ...), custom_call_target="tpu_custom_call" | custom-call | flops 12884901888 | bytes 31457280 | tf_op jit(solution)/shard_map/correlate/pallas_call | solution.py:267
  405.4 18.7 %correlate.4.refs_4_ = bf16[16,2,1024,1024]{3,2,1,0:T(8,128)(2,1)} custom-call(bf16[32,1280,128]{2,1,0:T(8,128)(2,1)} %all-to-all-done.refs_0_.refs_1_.refs_2_.refs_3_, bf16[32,1280,128]{2,1,0:T(8,128)(2,1)} %all-to-all-done.refs_0_.refs_1_.refs_2_.refs_3_, ...), custom_call_target="tpu_custom_call", output_to_operand_aliasing={{}: (4, {})} | custom-call | flops 17179869184 | bytes 41943040 | tf_op jit(solution)/shard_map/correlate/pallas_call | solution.py:267
  424.1 4.2 all-to-all-done.1.refs_1_.refs_2_.refs_3_
  428.2 7.2 %correlate.5 = bf16[16,2,1024,1024]{3,2,1,0:T(8,128)(2,1)} custom-call(bf16[32,1280,128]{2,1,0:T(8,128)(2,1)} %all-to-all-done.refs_0_.refs_1_.refs_2_.refs_3_, bf16[32,192,128]{2,1,0:T(8,128)(2,1)} %all-to-all-done.1.refs_1_.refs_2_.refs_3_, bf16[32,192,128]{2,1,0:T(8,128)(2,1)} %all-to-all-done.1.refs_1_.refs_2_.refs_3_, ...), custom_call_target="tpu_custom_call", output_to_operand_aliasing={{}: (4, {})} | custom-call | flops 4294967296 | bytes 10485760 | tf_op jit(solution)/shard_map/correlate/pallas_call | solution.py:267
Async XLA Ops:
  1.6 45.3 %collective-permute-start = (bf16[128,7168]{1,0:T(8,128)(2,1)S(1)}, bf16[128,7168]{1,0:T(8,128)(2,1)}, u32[]{:S(2)}, u32[]{:S(2)}) collective-permute-start(bf16[128,7168]{1,0:T(8,128)(2,1)S(1)} %slice.3), channel_id=1, source_target_pairs={{0,1},{1,2},{2,3},{4,5},{5,6},{6,7},{8,9},{9,10},{10,11},{12,13},{... | collective-permute-start | bytes 5505032 | tf_op jit(solution)/shard_map/ppermute | solution.py:21
  37.8 109.6 %all-to-all-start.2 = ((bf16[32,576,128]{2,1,0:T(8,128)(2,1)}), bf16[32,576,128]{2,1,0:T(8,128)(2,1)}, u32[]{:S(2)}, u32[]{:S(2)}) async-start(bf16[32,576,128]{2,1,0:T(8,128)(2,1)} %dft.7), calls=%async_computation.2 | async-start | bytes 9437184 | tf_op jit(solution)/shard_map/all_to_all | solution.py:295
  147.4 239.5 %all-to-all-start = ((bf16[32,1280,128]{2,1,0:T(8,128)(2,1)}), bf16[32,1280,128]{2,1,0:T(8,128)(2,1)}, u32[]{:S(2)}, u32[]{:S(2)}) async-start(bf16[32,1280,128]{2,1,0:T(8,128)(2,1)} %dft.5), calls=%async_computation | async-start | bytes 20971520 | tf_op jit(solution)/shard_map/all_to_all | solution.py:295
  386.9 41.3 %all-to-all-start.1 = ((bf16[32,192,128]{2,1,0:T(8,128)(2,1)}), bf16[32,192,128]{2,1,0:T(8,128)(2,1)}, u32[]{:S(2)}, u32[]{:S(2)}) async-start(bf16[32,192,128]{2,1,0:T(8,128)(2,1)} %dft.6), calls=%async_computation.1 | async-start | bytes 3145728 | tf_op jit(solution)/shard_map/all_to_all | solution.py:295

commit v7 on v4

--- a/solution.py
+++ b/solution.py
@@ -179,13 +179,11 @@
     )(*operands)
 
 
-def pipelined(block, count, fill, o_ref, slots):
-    step = pl.program_id(0)
-    depth, inputs = slots[0][0].shape
+def interleaved(block, fill, o_ref, right, left, across):
+    depth, inputs = right.shape
     spectra = depth // 2
 
-    def prepare(at, slot):
-        right, left, across = slot
+    def prepare(at):
         columns = pl.ds(at, block)
         fill(at, right)
         power = jnp.zeros((ROWS, block), jnp.float32)
@@ -196,9 +194,8 @@
         across[:, columns] = jnp.broadcast_to(scale, (8, block))
         left[columns, :] = right[:, columns].T
 
-    def multiply(at, slot):
-        right, left, across = slot
-        rows, columns = pl.ds(at, block), pl.ds(at, inputs - at)
+    def multiply(at):
+        rows, columns = pl.ds(at, block), pl.ds(0, at + block)
         own = left[rows, :]
         swapped = jnp.concatenate([own[:, spectra:], -own[:, :spectra]], axis=1)
         down = across[:, rows].T[:, :1]
@@ -206,29 +203,21 @@
             gram = jnp.dot(operand, right[:, columns], preferred_element_type=jnp.float32)
             scaled = (gram * down * across[:1, columns]).astype(jnp.bfloat16)
             o_ref[0, part, rows, columns] = scaled
-            for below in range(at + block, inputs, block):
-                mirror = scaled[:, below - at : below - at + block].T
-                o_ref[0, part, pl.ds(below, block), rows] = -mirror if part else mirror
-
-    def both(old, new):
-        for at in range(0, inputs, block):
-            if old is not None:
-                multiply(at, old)
-            if new is not None:
-                prepare(at, new)
-
-    even, odd = slots
-    inside = (step > 0) & (step < count)
-    pl.when(step == 0)(lambda: both(None, even))
-    pl.when(inside & (step % 2 == 1))(lambda: both(even, odd))
-    pl.when(inside & (step % 2 == 0))(lambda: both(odd, even))
-    pl.when(step == count)(lambda: both(slots[(count - 1) % 2], None))
-
-
-def correlate_kernel(block, count, slabs, blocks, *refs):
-    sources, o_ref, slots = refs[:blocks], refs[-7], (refs[-6:-3], refs[-3:])
+            for before in range(0, at, block):
+                mirror = scaled[:, before : before + block].T
+                o_ref[0, part, pl.ds(before, block), rows] = -mirror if part else mirror
+
+    prepare(0)
+    for at in range(0, inputs, block):
+        multiply(at)
+        if at + block < inputs:
+            prepare(at + block)
+
+
+def correlate_kernel(block, slabs, blocks, *refs):
+    sources, o_ref, scratch = refs[:blocks], refs[-4], refs[-3:]
     devices, _, width = sources[0].shape
-    spectra = slots[0][0].shape[0] // 2
+    spectra = scratch[0].shape[0] // 2
 
     def fill(first, right):
         for part in range(2):
@@ -240,15 +229,15 @@
                         device, pl.ds(part * ROWS, ROWS), :
                     ]
 
-    pipelined(block, count, fill, o_ref, slots)
-
-
-def plain_correlate_kernel(block, count, r_ref, o_ref, *scratch):
+    interleaved(block, fill, o_ref, *scratch)
+
+
+def plain_correlate_kernel(block, r_ref, o_ref, *scratch):
     def fill(first, right):
         columns = pl.ds(first, block)
         right[:, columns] = r_ref[0, :, columns]
 
-    pipelined(block, count, fill, o_ref, (scratch[:3], scratch[3:]))
+    interleaved(block, fill, o_ref, *scratch)
 
 
 def correlate(kernel, in_specs, operands, total, first, count, out_shape, spectra):
@@ -258,21 +247,19 @@
         aliases = {len(operands): 0}
         in_specs = [*in_specs, pl.BlockSpec(memory_space=pl.ANY)]
         operands = [*operands, total]
-    slot = [
+    scratch = [
         pltpu.VMEM((2 * spectra, inputs), jnp.bfloat16),
         pltpu.VMEM((inputs, 2 * spectra), jnp.bfloat16),
         pltpu.VMEM((8, inputs), jnp.float32),
     ]
     return pl.pallas_call(
         kernel,
-        grid=(count + 1,),
+        grid=(count,),
         in_specs=in_specs,
-        out_specs=pl.BlockSpec(
-            (1, 2, inputs, inputs), lambda c: (first + jnp.maximum(c - 1, 0), 0, 0, 0)
-        ),
+        out_specs=pl.BlockSpec((1, 2, inputs, inputs), lambda c: (first + c, 0, 0, 0)),
         out_shape=out_shape,
         input_output_aliases=aliases,
-        scratch_shapes=slot + slot,
+        scratch_shapes=scratch,
         compiler_params=pltpu.CompilerParams(vmem_limit_bytes=VMEM),
         cost_estimate=pl.CostEstimate(
             flops=8 * count * inputs * inputs * spectra,
@@ -310,12 +297,8 @@
     depth = 2 * slabs * spectra
     planes = turned.transpose(2, 3, 1, 4, 0, 5).reshape(channels, depth, groups * inputs)
     return correlate(
-        functools.partial(plain_correlate_kernel, min(256, groups * inputs), channels),
-        [
-            pl.BlockSpec(
-                (1, depth, groups * inputs), lambda c: (jnp.minimum(c, channels - 1), 0, 0)
-            )
-        ],
+        functools.partial(plain_correlate_kernel, min(256, groups * inputs)),
+        [pl.BlockSpec((1, depth, groups * inputs), lambda c: (c, 0, 0))],
         [planes],
         None,
         0,
@@ -370,16 +353,11 @@
     ):
         bases = [first] + [base + b * count for b in range(blocks - 1)]
         in_specs = [
-            pl.BlockSpec(
-                (devices, unit, inputs),
-                lambda c, at=at, end=count - 1: (0, at + jnp.minimum(c, end), 0),
-            )
+            pl.BlockSpec((devices, unit, inputs), lambda c, at=at: (0, at + c, 0))
             for at in bases
         ]
         operands = [middle_turned] + [turned] * (blocks - 1)
-        kernel = functools.partial(
-            correlate_kernel, min(256, total_inputs), count, slabs, blocks
-        )
+        kernel = functools.partial(correlate_kernel, min(256, total_inputs), slabs, blocks)
         total = correlate(
             kernel, in_specs, operands, total, first, count, out_shape, slabs * spectra
         )

time: 434 us -> 434 us (level)
  no operation moved by 1% of the time
where the time goes in v7:
time: 434 us; the launch traced here: 432 us
  waiting for transfers between devices  288 us (66%)
  Pallas kernels  115 us (26%)
  starting transfers between devices  27.8 us (6%)
    all_to_all x3, waiting for transfers between devices, exchange(): lax.all_to_all(rows, ('inp', 'tm'), split_axis=0, concat_axis=0, tiled=True)  282 us
    pallas_call x4, Pallas kernels, transform(): pl.pallas_call(functools.partial(dft_kernel, inputs), grid=(spectra // RO...  46.2 us
    pallas_call x3, Pallas kernels, correlate(): pl.pallas_call(kernel, grid=(count,), in_specs=in_specs, out_specs=pl.Blo...  40.5 us
    all_to_all x3, starting transfers between devices, exchange(): lax.all_to_all(rows, ('inp', 'tm'), split_axis=0, concat_axis=0, tiled=True)  21.6 us
    pallas_call x1, Pallas kernels, filter_main(): pl.pallas_call(functools.partial(main_filter_kernel, taps, frame, spectra...  18.6 us
    pallas_call x1, Pallas kernels, filter_edge(): pl.pallas_call(functools.partial(edge_filter_kernel, taps, frame, ROWS),...  9.38 us
  transfers between devices with their start and end apart: 4, of which 4 were waited for; matrix products, arithmetic and copies ran while one was open for 0% of the time, Pallas kernels for 25%

profile of v7, /device:TPU:0, one launch (start us, length us, event | category | flops | bytes accessed | tf_op | source)
XLA Modules:
  0.0 431.7 jit_solution(16864912405227431856)
XLA Ops:
  0.0 1.6 slice.3
  1.6 6.2 %collective-permute-start = (bf16[128,7168]{1,0:T(8,128)(2,1)S(1)}, bf16[128,7168]{1,0:T(8,128)(2,1)}, u32[]{:S(2)}, u32[]{:S(2)}) collective-permute-start(bf16[128,7168]{1,0:T(8,128)(2,1)S(1)} %slice.3), channel_id=1, source_target_pairs={{0,1},{1,2},{2,3},{4,5},{5,6},{6,7},{8,9},{9,10},{10,11},{12,13},{... | collective-permute-start | bytes 5505032 | tf_op jit(solution)/shard_map/ppermute | solution.py:21
  7.8 18.6 %filter_main.1.f_ref = bf16[48,128,1024]{2,1,0:T(8,128)(2,1)} custom-call(bf16[128,65536]{1,0:T(8,128)(2,1)} %v_ref.3, f32[8,1024]{1,0:T(8,128)} %p_ref.3), custom_call_target="tpu_custom_call" | custom-call | flops 134217728 | bytes 33554432 | tf_op jit(solution)/shard_map/filter_main/pallas_call | solution.py:88
  26.4 11.4 %dft.7 = bf16[32,576,128]{2,1,0:T(8,128)(2,1)} custom-call(bf16[384,1024]{1,0:T(8,128)(2,1)} %constant.8.clone.t_ref, bf16[48,128,1024]{2,1,0:T(8,128)(2,1)} %filter_main.1.f_ref), custom_call_target="tpu_custom_call" | custom-call | flops 19327352832 | bytes 17301504 | tf_op jit(solution)/shard_map/dft/pallas_call | solution.py:162
  37.8 3.7 all-to-all-start.2
  41.5 5.5 %collective-permute-done.e_ref = bf16[128,7168]{1,0:T(8,128)(2,1)} collective-permute-done((bf16[128,7168]{1,0:T(8,128)(2,1)S(1)}, bf16[128,7168]{1,0:T(8,128)(2,1)}, u32[]{:S(2)}, u32[]{:S(2)}) %collective-permute-start) | collective-permute-done | bytes 1835040 | tf_op jit(solution)/shard_map/ppermute | solution.py:21
  47.0 9.4 %filter_edge.1.f_ref = bf16[16,128,1024]{2,1,0:T(8,128)(2,1)} custom-call(bf16[128,65536]{1,0:T(8,128)(2,1)} %v_ref.3, bf16[128,7168]{1,0:T(8,128)(2,1)} %collective-permute-done.e_ref, f32[8,1024]{1,0:T(8,128)} %p_ref.3), custom_call_target="tpu_custom_call" | custom-call | flops 68719476736 | bytes 12582912 | tf_op jit(solution)/shard_map/filter_edge/pallas_call | solution.py:110
  56.3 10.0 %dft.4.refs_0_ = bf16[32,1280,128]{2,1,0:T(8,128)(2,1)} custom-call(bf16[1024,1024]{1,0:T(8,128)(2,1)} %constant.9.clone.t_ref, bf16[16,128,1024]{2,1,0:T(8,128)(2,1)} %filter_edge.1.f_ref), custom_call_target="tpu_custom_call" | custom-call | flops 17179869184 | bytes 8388608 | tf_op jit(solution)/shard_map/dft/pallas_call | solution.py:162
  66.4 16.1 %dft.5 = bf16[32,1280,128]{2,1,0:T(8,128)(2,1)} custom-call(bf16[512,1024]{1,0:T(8,128)(2,1)} %constant.10.clone.t_ref, bf16[48,128,1024]{2,1,0:T(8,128)(2,1)} %filter_main.1.f_ref, bf16[32,1280,128]{2,1,0:T(8,128)(2,1)} %dft.4.refs_0_), custom_call_target="tpu_custom_call", output_to_operand_aliasing={{}: (2, {})} | custom-call | flops 25769803776 | bytes 18874368 | tf_op jit(solution)/shard_map/dft/pallas_call | solution.py:162
  82.4 62.4 %all-to-all-done.2.refs_1_.refs_2_.refs_3_ = bf16[32,576,128]{2,1,0:T(8,128)(2,1)} async-done(((bf16[32,576,128]{2,1,0:T(8,128)(2,1)}), bf16[32,576,128]{2,1,0:T(8,128)(2,1)}, u32[]{:S(2)}, u32[]{:S(2)}) %all-to-all-start.2) | async-done | bytes 4718624 | tf_op jit(solution)/shard_map/all_to_all | solution.py:280
  144.9 7.8 %all-to-all-start = ((bf16[32,1280,128]{2,1,0:T(8,128)(2,1)}), bf16[32,1280,128]{2,1,0:T(8,128)(2,1)}, u32[]{:S(2)}, u32[]{:S(2)}) async-start(bf16[32,1280,128]{2,1,0:T(8,128)(2,1)} %dft.5), calls=%async_computation | async-start | bytes 20971520 | tf_op jit(solution)/shard_map/all_to_all | solution.py:280
  152.7 8.7 %dft.6 = bf16[32,192,128]{2,1,0:T(8,128)(2,1)} custom-call(bf16[128,1024]{1,0:T(8,128)(2,1)} %constant.11.clone.t_ref, bf16[48,128,1024]{2,1,0:T(8,128)(2,1)} %filter_main.1.f_ref), custom_call_target="tpu_custom_call" | custom-call | flops 6442450944 | bytes 14155776 | tf_op jit(solution)/shard_map/dft/pallas_call | solution.py:162
  161.4 217.4 %all-to-all-done.refs_0_.refs_1_.refs_2_.refs_3_ = bf16[32,1280,128]{2,1,0:T(8,128)(2,1)} async-done(((bf16[32,1280,128]{2,1,0:T(8,128)(2,1)}), bf16[32,1280,128]{2,1,0:T(8,128)(2,1)}, u32[]{:S(2)}, u32[]{:S(2)}) %all-to-all-start) | async-done | bytes 10485792 | tf_op jit(solution)/shard_map/all_to_all | solution.py:280
  378.9 10.1 %all-to-all-start.1 = ((bf16[32,192,128]{2,1,0:T(8,128)(2,1)}), bf16[32,192,128]{2,1,0:T(8,128)(2,1)}, u32[]{:S(2)}, u32[]{:S(2)}) async-start(bf16[32,192,128]{2,1,0:T(8,128)(2,1)} %dft.6), calls=%async_computation.1 | async-start | bytes 3145728 | tf_op jit(solution)/shard_map/all_to_all | solution.py:280
  388.9 14.8 %correlate.3.refs_4_ = bf16[16,2,1024,1024]{3,2,1,0:T(8,128)(2,1)} custom-call(bf16[32,1280,128]{2,1,0:T(8,128)(2,1)} %all-to-all-done.refs_0_.refs_1_.refs_2_.refs_3_, bf16[32,576,128]{2,1,0:T(8,128)(2,1)} %all-to-all-done.2.refs_1_.refs_2_.refs_3_, bf16[32,576,128]{2,1,0:T(8,128)(2,1)} %all-to-all-done.2.refs_1_.refs_2_.refs_3_, ...), custom_call_target="tpu_custom_call" | custom-call | flops 12884901888 | bytes 31457280 | tf_op jit(solution)/shard_map/correlate/pallas_call | solution.py:255
  403.8 18.7 %correlate.4.refs_4_ = bf16[16,2,1024,1024]{3,2,1,0:T(8,128)(2,1)} custom-call(bf16[32,1280,128]{2,1,0:T(8,128)(2,1)} %all-to-all-done.refs_0_.refs_1_.refs_2_.refs_3_, bf16[32,1280,128]{2,1,0:T(8,128)(2,1)} %all-to-all-done.refs_0_.refs_1_.refs_2_.refs_3_, ...), custom_call_target="tpu_custom_call", output_to_operand_aliasing={{}: (4, {})} | custom-call | flops 17179869184 | bytes 41943040 | tf_op jit(solution)/shard_map/correlate/pallas_call | solution.py:255
  422.5 2.2 all-to-all-done.1.refs_1_.refs_2_.refs_3_
  424.7 7.0 %correlate.5 = bf16[16,2,1024,1024]{3,2,1,0:T(8,128)(2,1)} custom-call(bf16[32,1280,128]{2,1,0:T(8,128)(2,1)} %all-to-all-done.refs_0_.refs_1_.refs_2_.refs_3_, bf16[32,192,128]{2,1,0:T(8,128)(2,1)} %all-to-all-done.1.refs_1_.refs_2_.refs_3_, bf16[32,192,128]{2,1,0:T(8,128)(2,1)} %all-to-all-done.1.refs_1_.refs_2_.refs_3_, ...), custom_call_target="tpu_custom_call", output_to_operand_aliasing={{}: (4, {})} | custom-call | flops 4294967296 | bytes 10485760 | tf_op jit(solution)/shard_map/correlate/pallas_call | solution.py:255
Async XLA Ops:
  1.6 45.3 %collective-permute-start = (bf16[128,7168]{1,0:T(8,128)(2,1)S(1)}, bf16[128,7168]{1,0:T(8,128)(2,1)}, u32[]{:S(2)}, u32[]{:S(2)}) collective-permute-start(bf16[128,7168]{1,0:T(8,128)(2,1)S(1)} %slice.3), channel_id=1, source_target_pairs={{0,1},{1,2},{2,3},{4,5},{5,6},{6,7},{8,9},{9,10},{10,11},{12,13},{... | collective-permute-start | bytes 5505032 | tf_op jit(solution)/shard_map/ppermute | solution.py:21
  37.8 107.1 %all-to-all-start.2 = ((bf16[32,576,128]{2,1,0:T(8,128)(2,1)}), bf16[32,576,128]{2,1,0:T(8,128)(2,1)}, u32[]{:S(2)}, u32[]{:S(2)}) async-start(bf16[32,576,128]{2,1,0:T(8,128)(2,1)} %dft.7), calls=%async_computation.2 | async-start | bytes 9437184 | tf_op jit(solution)/shard_map/all_to_all | solution.py:280
  144.9 234.0 %all-to-all-start = ((bf16[32,1280,128]{2,1,0:T(8,128)(2,1)}), bf16[32,1280,128]{2,1,0:T(8,128)(2,1)}, u32[]{:S(2)}, u32[]{:S(2)}) async-start(bf16[32,1280,128]{2,1,0:T(8,128)(2,1)} %dft.5), calls=%async_computation | async-start | bytes 20971520 | tf_op jit(solution)/shard_map/all_to_all | solution.py:280
  378.9 45.8 %all-to-all-start.1 = ((bf16[32,192,128]{2,1,0:T(8,128)(2,1)}), bf16[32,192,128]{2,1,0:T(8,128)(2,1)}, u32[]{:S(2)}, u32[]{:S(2)}) async-start(bf16[32,192,128]{2,1,0:T(8,128)(2,1)} %dft.6), calls=%async_computation.1 | async-start | bytes 3145728 | tf_op jit(solution)/shard_map/all_to_all | solution.py:280

commit v8 on v7

--- a/solution.py
+++ b/solution.py
@@ -194,24 +194,31 @@
         across[:, columns] = jnp.broadcast_to(scale, (8, block))
         left[columns, :] = right[:, columns].T
 
-    def multiply(at):
+    def multiply(at, part):
         rows, columns = pl.ds(at, block), pl.ds(0, at + block)
-        own = left[rows, :]
-        swapped = jnp.concatenate([own[:, spectra:], -own[:, :spectra]], axis=1)
+        operand = left[rows, :]
+        if part:
+            operand = jnp.concatenate([operand[:, spectra:], -operand[:, :spectra]], axis=1)
         down = across[:, rows].T[:, :1]
-        for part, operand in enumerate((own, swapped)):
-            gram = jnp.dot(operand, right[:, columns], preferred_element_type=jnp.float32)
-            scaled = (gram * down * across[:1, columns]).astype(jnp.bfloat16)
-            o_ref[0, part, rows, columns] = scaled
-            for before in range(0, at, block):
-                mirror = scaled[:, before : before + block].T
-                o_ref[0, part, pl.ds(before, block), rows] = -mirror if part else mirror
-
-    prepare(0)
-    for at in range(0, inputs, block):
-        multiply(at)
-        if at + block < inputs:
-            prepare(at + block)
+        gram = jnp.dot(operand, right[:, columns], preferred_element_type=jnp.float32)
+        scaled = (gram * down * across[:1, columns]).astype(jnp.bfloat16)
+        o_ref[0, 0, rows, columns] = scaled
+        for before in range(0, at, block):
+            mirror = scaled[:, before : before + block].T
+            o_ref[0, 0, pl.ds(before, block), rows] = -mirror if part else mirror
+
+    @pl.when(pl.program_id(1) == 0)
+    def _():
+        prepare(0)
+        for at in range(0, inputs, block):
+            multiply(at, 0)
+            if at + block < inputs:
+                prepare(at + block)
+
+    @pl.when(pl.program_id(1) == 1)
+    def _():
+        for at in range(0, inputs, block):
+            multiply(at, 1)
 
 
 def correlate_kernel(block, slabs, blocks, *refs):
@@ -254,9 +261,9 @@
     ]
     return pl.pallas_call(
         kernel,
-        grid=(count,),
+        grid=(count, 2),
         in_specs=in_specs,
-        out_specs=pl.BlockSpec((1, 2, inputs, inputs), lambda c: (first + c, 0, 0, 0)),
+        out_specs=pl.BlockSpec((1, 1, inputs, inputs), lambda c, part: (first + c, part, 0, 0)),
         out_shape=out_shape,
         input_output_aliases=aliases,
         scratch_shapes=scratch,
@@ -298,7 +305,7 @@
     planes = turned.transpose(2, 3, 1, 4, 0, 5).reshape(channels, depth, groups * inputs)
     return correlate(
         functools.partial(plain_correlate_kernel, min(256, groups * inputs)),
-        [pl.BlockSpec((1, depth, groups * inputs), lambda c: (c, 0, 0))],
+        [pl.BlockSpec((1, depth, groups * inputs), lambda c, part: (c, 0, 0))],
         [planes],
         None,
         0,
@@ -353,7 +360,7 @@
     ):
         bases = [first] + [base + b * count for b in range(blocks - 1)]
         in_specs = [
-            pl.BlockSpec((devices, unit, inputs), lambda c, at=at: (0, at + c, 0))
+            pl.BlockSpec((devices, unit, inputs), lambda c, part, at=at: (0, at + c, 0))
             for at in bases
         ]
         operands = [middle_turned] + [turned] * (blocks - 1)

time: 434 us -> 448 us (1.032)
  Pallas kernels: 115 us -> 132 us
    pallas_call x3, Pallas kernels: 40.5 us -> 57.4 us  [correlate(): pl.pallas_call(kernel, grid=(count, 2), in_specs=in_specs, out_specs=pl.B...]
  transfers between devices with their start and end apart: 4 -> 4, of which waited for: 4 -> 3; matrix products, arithmetic and copies ran while one was open for 0% -> 0% of each run, Pallas kernels for 25% -> 28%
where the time goes in v8:
time: 448 us; the launch traced here: 446 us
  waiting for transfers between devices  285 us (64%)
  Pallas kernels  132 us (29%)
  starting transfers between devices  27.8 us (6%)
    all_to_all x3, waiting for transfers between devices, exchange(): lax.all_to_all(rows, ('inp', 'tm'), split_axis=0, concat_axis=0, tiled=True)  280 us
    pallas_call x3, Pallas kernels, correlate(): pl.pallas_call(kernel, grid=(count, 2), in_specs=in_specs, out_specs=pl.B...  57.4 us
    pallas_call x4, Pallas kernels, transform(): pl.pallas_call(functools.partial(dft_kernel, inputs), grid=(spectra // RO...  46.2 us
    all_to_all x3, starting transfers between devices, exchange(): lax.all_to_all(rows, ('inp', 'tm'), split_axis=0, concat_axis=0, tiled=True)  21.6 us
    pallas_call x1, Pallas kernels, filter_main(): pl.pallas_call(functools.partial(main_filter_kernel, taps, frame, spectra...  18.6 us
    pallas_call x1, Pallas kernels, filter_edge(): pl.pallas_call(functools.partial(edge_filter_kernel, taps, frame, ROWS),...  9.38 us
  transfers between devices with their start and end apart: 4, of which 3 were waited for; matrix products, arithmetic and copies ran while one was open for 0% of the time, Pallas kernels for 28%

profile of v8, /device:TPU:0, one launch (start us, length us, event | category | flops | bytes accessed | tf_op | source)
XLA Modules:
  0.0 446.3 jit_solution(7459765145240775242)
XLA Ops:
  0.0 1.6 slice.3
  1.6 6.2 %collective-permute-start = (bf16[128,7168]{1,0:T(8,128)(2,1)S(1)}, bf16[128,7168]{1,0:T(8,128)(2,1)}, u32[]{:S(2)}, u32[]{:S(2)}) collective-permute-start(bf16[128,7168]{1,0:T(8,128)(2,1)S(1)} %slice.3), channel_id=1, source_target_pairs={{0,1},{1,2},{2,3},{4,5},{5,6},{6,7},{8,9},{9,10},{10,11},{12,13},{... | collective-permute-start | bytes 5505032 | tf_op jit(solution)/shard_map/ppermute | solution.py:21
  7.8 18.6 %filter_main.1.f_ref = bf16[48,128,1024]{2,1,0:T(8,128)(2,1)} custom-call(bf16[128,65536]{1,0:T(8,128)(2,1)} %v_ref.3, f32[8,1024]{1,0:T(8,128)} %p_ref.3), custom_call_target="tpu_custom_call" | custom-call | flops 134217728 | bytes 33554432 | tf_op jit(solution)/shard_map/filter_main/pallas_call | solution.py:88
  26.4 11.4 %dft.7 = bf16[32,576,128]{2,1,0:T(8,128)(2,1)} custom-call(bf16[384,1024]{1,0:T(8,128)(2,1)} %constant.8.clone.t_ref, bf16[48,128,1024]{2,1,0:T(8,128)(2,1)} %filter_main.1.f_ref), custom_call_target="tpu_custom_call" | custom-call | flops 19327352832 | bytes 17301504 | tf_op jit(solution)/shard_map/dft/pallas_call | solution.py:162
  37.8 3.7 all-to-all-start.2
  41.5 5.5 %collective-permute-done.e_ref = bf16[128,7168]{1,0:T(8,128)(2,1)} collective-permute-done((bf16[128,7168]{1,0:T(8,128)(2,1)S(1)}, bf16[128,7168]{1,0:T(8,128)(2,1)}, u32[]{:S(2)}, u32[]{:S(2)}) %collective-permute-start) | collective-permute-done | bytes 1835040 | tf_op jit(solution)/shard_map/ppermute | solution.py:21
  47.0 9.4 %filter_edge.1.f_ref = bf16[16,128,1024]{2,1,0:T(8,128)(2,1)} custom-call(bf16[128,65536]{1,0:T(8,128)(2,1)} %v_ref.3, bf16[128,7168]{1,0:T(8,128)(2,1)} %collective-permute-done.e_ref, f32[8,1024]{1,0:T(8,128)} %p_ref.3), custom_call_target="tpu_custom_call" | custom-call | flops 68719476736 | bytes 12582912 | tf_op jit(solution)/shard_map/filter_edge/pallas_call | solution.py:110
  56.3 10.0 %dft.4.refs_0_ = bf16[32,1280,128]{2,1,0:T(8,128)(2,1)} custom-call(bf16[1024,1024]{1,0:T(8,128)(2,1)} %constant.9.clone.t_ref, bf16[16,128,1024]{2,1,0:T(8,128)(2,1)} %filter_edge.1.f_ref), custom_call_target="tpu_custom_call" | custom-call | flops 17179869184 | bytes 8388608 | tf_op jit(solution)/shard_map/dft/pallas_call | solution.py:162
  66.4 16.1 %dft.5 = bf16[32,1280,128]{2,1,0:T(8,128)(2,1)} custom-call(bf16[512,1024]{1,0:T(8,128)(2,1)} %constant.10.clone.t_ref, bf16[48,128,1024]{2,1,0:T(8,128)(2,1)} %filter_main.1.f_ref, bf16[32,1280,128]{2,1,0:T(8,128)(2,1)} %dft.4.refs_0_), custom_call_target="tpu_custom_call", output_to_operand_aliasing={{}: (2, {})} | custom-call | flops 25769803776 | bytes 18874368 | tf_op jit(solution)/shard_map/dft/pallas_call | solution.py:162
  82.4 62.4 %all-to-all-done.2.refs_1_.refs_2_.refs_3_ = bf16[32,576,128]{2,1,0:T(8,128)(2,1)} async-done(((bf16[32,576,128]{2,1,0:T(8,128)(2,1)}), bf16[32,576,128]{2,1,0:T(8,128)(2,1)}, u32[]{:S(2)}, u32[]{:S(2)}) %all-to-all-start.2) | async-done | bytes 4718624 | tf_op jit(solution)/shard_map/all_to_all | solution.py:287
  144.9 7.8 %all-to-all-start = ((bf16[32,1280,128]{2,1,0:T(8,128)(2,1)}), bf16[32,1280,128]{2,1,0:T(8,128)(2,1)}, u32[]{:S(2)}, u32[]{:S(2)}) async-start(bf16[32,1280,128]{2,1,0:T(8,128)(2,1)} %dft.5), calls=%async_computation | async-start | bytes 20971520 | tf_op jit(solution)/shard_map/all_to_all | solution.py:287
  152.7 8.7 %dft.6 = bf16[32,192,128]{2,1,0:T(8,128)(2,1)} custom-call(bf16[128,1024]{1,0:T(8,128)(2,1)} %constant.11.clone.t_ref, bf16[48,128,1024]{2,1,0:T(8,128)(2,1)} %filter_main.1.f_ref), custom_call_target="tpu_custom_call" | custom-call | flops 6442450944 | bytes 14155776 | tf_op jit(solution)/shard_map/dft/pallas_call | solution.py:162
  161.4 217.4 %all-to-all-done.refs_0_.refs_1_.refs_2_.refs_3_ = bf16[32,1280,128]{2,1,0:T(8,128)(2,1)} async-done(((bf16[32,1280,128]{2,1,0:T(8,128)(2,1)}), bf16[32,1280,128]{2,1,0:T(8,128)(2,1)}, u32[]{:S(2)}, u32[]{:S(2)}) %all-to-all-start) | async-done | bytes 10485792 | tf_op jit(solution)/shard_map/all_to_all | solution.py:287
  378.9 10.1 %all-to-all-start.1 = ((bf16[32,192,128]{2,1,0:T(8,128)(2,1)}), bf16[32,192,128]{2,1,0:T(8,128)(2,1)}, u32[]{:S(2)}, u32[]{:S(2)}) async-start(bf16[32,192,128]{2,1,0:T(8,128)(2,1)} %dft.6), calls=%async_computation.1 | async-start | bytes 3145728 | tf_op jit(solution)/shard_map/all_to_all | solution.py:287
  388.9 21.4 %correlate.3.refs_4_ = bf16[16,2,1024,1024]{3,2,1,0:T(8,128)(2,1)} custom-call(bf16[32,1280,128]{2,1,0:T(8,128)(2,1)} %all-to-all-done.refs_0_.refs_1_.refs_2_.refs_3_, bf16[32,576,128]{2,1,0:T(8,128)(2,1)} %all-to-all-done.2.refs_1_.refs_2_.refs_3_, bf16[32,576,128]{2,1,0:T(8,128)(2,1)} %all-to-all-done.2.refs_1_.refs_2_.refs_3_, ...), custom_call_target="tpu_custom_call" | custom-call | flops 12884901888 | bytes 31457280 | tf_op jit(solution)/shard_map/correlate/pallas_call | solution.py:262
  410.3 27.8 %correlate.4.refs_4_ = bf16[16,2,1024,1024]{3,2,1,0:T(8,128)(2,1)} custom-call(bf16[32,1280,128]{2,1,0:T(8,128)(2,1)} %all-to-all-done.refs_0_.refs_1_.refs_2_.refs_3_, bf16[32,1280,128]{2,1,0:T(8,128)(2,1)} %all-to-all-done.refs_0_.refs_1_.refs_2_.refs_3_, ...), custom_call_target="tpu_custom_call", output_to_operand_aliasing={{}: (4, {})} | custom-call | flops 17179869184 | bytes 41943040 | tf_op jit(solution)/shard_map/correlate/pallas_call | solution.py:262
  438.1 0.0 all-to-all-done.1.refs_1_.refs_2_.refs_3_
  438.1 8.2 %correlate.5 = bf16[16,2,1024,1024]{3,2,1,0:T(8,128)(2,1)} custom-call(bf16[32,1280,128]{2,1,0:T(8,128)(2,1)} %all-to-all-done.refs_0_.refs_1_.refs_2_.refs_3_, bf16[32,192,128]{2,1,0:T(8,128)(2,1)} %all-to-all-done.1.refs_1_.refs_2_.refs_3_, bf16[32,192,128]{2,1,0:T(8,128)(2,1)} %all-to-all-done.1.refs_1_.refs_2_.refs_3_, ...), custom_call_target="tpu_custom_call", output_to_operand_aliasing={{}: (4, {})} | custom-call | flops 4294967296 | bytes 10485760 | tf_op jit(solution)/shard_map/correlate/pallas_call | solution.py:262
Async XLA Ops:
  1.6 45.3 %collective-permute-start = (bf16[128,7168]{1,0:T(8,128)(2,1)S(1)}, bf16[128,7168]{1,0:T(8,128)(2,1)}, u32[]{:S(2)}, u32[]{:S(2)}) collective-permute-start(bf16[128,7168]{1,0:T(8,128)(2,1)S(1)} %slice.3), channel_id=1, source_target_pairs={{0,1},{1,2},{2,3},{4,5},{5,6},{6,7},{8,9},{9,10},{10,11},{12,13},{... | collective-permute-start | bytes 5505032 | tf_op jit(solution)/shard_map/ppermute | solution.py:21
  37.8 107.1 %all-to-all-start.2 = ((bf16[32,576,128]{2,1,0:T(8,128)(2,1)}), bf16[32,576,128]{2,1,0:T(8,128)(2,1)}, u32[]{:S(2)}, u32[]{:S(2)}) async-start(bf16[32,576,128]{2,1,0:T(8,128)(2,1)} %dft.7), calls=%async_computation.2 | async-start | bytes 9437184 | tf_op jit(solution)/shard_map/all_to_all | solution.py:287
  144.9 234.0 %all-to-all-start = ((bf16[32,1280,128]{2,1,0:T(8,128)(2,1)}), bf16[32,1280,128]{2,1,0:T(8,128)(2,1)}, u32[]{:S(2)}, u32[]{:S(2)}) async-start(bf16[32,1280,128]{2,1,0:T(8,128)(2,1)} %dft.5), calls=%async_computation | async-start | bytes 20971520 | tf_op jit(solution)/shard_map/all_to_all | solution.py:287
  378.9 59.2 %all-to-all-start.1 = ((bf16[32,192,128]{2,1,0:T(8,128)(2,1)}), bf16[32,192,128]{2,1,0:T(8,128)(2,1)}, u32[]{:S(2)}, u32[]{:S(2)}) async-start(bf16[32,192,128]{2,1,0:T(8,128)(2,1)} %dft.6), calls=%async_computation.1 | async-start | bytes 3145728 | tf_op jit(solution)/shard_map/all_to_all | solution.py:287
